TPU v7x, 32 devices: a whole 2x2x4 slice. The times are simulated.
32 devices in a mesh: tm: 4 (over y, core), height: 8 (over z, x).
Axes of the slice: x: 2, y: 2, z: 4, core: 2. Of those that a mesh axis runs over, the one named last changes fastest.
Arguments:
- queries: bfloat16 [4, 8, 2, 64, 3072], P('tm', 'height'), may hold values from -40 to 40
- keys_values: bfloat16 [4, 8, 2, 2, 64, 3072], P('tm', 'height'), may hold values from -6.2 to 6.2
- far_cubes: int32 [4, 8, 2, 24, 16], P('tm', 'height'), may hold values from 0 to 63, as said below
- out_weight: bfloat16 [3072, 3072], replicated, may hold values from -0.59765625 to 0.59765625
Outputs:
- output: bfloat16 [4, 8, 2, 64, 3072], P('tm', 'height')
Inputs may be any that keep to these rules, and one draw needn't show every extreme that they name: `far_cubes`: the 16 cubes of one list are distinct. Over all cubes that one device holds, the distinct pairs (far cube, head) whose cube lies on one given device number at most 16, and exactly 16 for some given devices, from every device.
All inputs are finite; a program needn't handle non-finite values.
Results may differ from a plain program's by a relative error of at most 0.0058.
Values may be sent and summed in bfloat16 or wider, within the bound.
No kernel may reach another device: no remote copies, remote signals or barrier semaphores. Data moves between devices by JAX's collectives and lax.ppermute only.
A program may use at most 256 MiB of HBM per device.

v0:
```python
import math

import jax
import jax.numpy as jnp
from jax import lax
from jax.sharding import PartitionSpec as P

HEADS = 24
SLOTS = 512


def padded_2(shard, sides, width):
    for axis, dim in sides:
        peers, length = (lax.axis_size(axis), shard.shape[dim])
        up = [(i, (i + 1) % peers) for i in range(peers - 1)]
        down = [(j, i) for i, j in up]
        last = lax.slice_in_dim(shard, length - width, length, axis=dim)
        leading = lax.slice_in_dim(shard, 0, width, axis=dim)
        before = lax.ppermute(last, axis, up)
        after = lax.ppermute(leading, axis, down)
        shard = jnp.concatenate([before, shard, after], axis=dim)
    return shard


def body(queries, keys_values, far_cubes, out_weight):
    tm_count = lax.axis_size("tm")
    height_count = lax.axis_size("height")
    device_count = tm_count * height_count
    capacity = SLOTS // device_count
    span_time, span_height, span_width, cube, width = queries.shape
    heads = HEADS
    head_size = width // heads
    far_count = far_cubes.shape[-1]
    local_count = span_time * span_height * span_width
    grid_time = span_time * tm_count
    grid_height = span_height * height_count
    far_ids = far_cubes.reshape(local_count, heads, far_count)
    far_time = far_ids // (grid_height * span_width)
    far_height = far_ids // span_width % grid_height
    far_width = far_ids % span_width
    owner_dev = far_time // span_time * height_count + far_height // span_height
    local_cube = (
        far_time % span_time * span_height + far_height % span_height
    ) * span_width + far_width
    tile_code = local_cube * heads + jnp.arange(heads, dtype=jnp.int32)[None, :, None]
    wanted = (
        jnp.zeros((device_count, local_count * heads), jnp.int32).at[owner_dev, tile_code].max(1)
    )
    slot_rank = jnp.cumsum(wanted, axis=1) - 1
    far_slot = owner_dev * capacity + slot_rank[owner_dev, tile_code]
    target = jnp.where(wanted > 0, slot_rank, capacity)
    columns = jnp.broadcast_to(
        jnp.arange(local_count * heads, dtype=jnp.int32)[None, :], wanted.shape
    )
    rows = jnp.broadcast_to(jnp.arange(device_count, dtype=jnp.int32)[:, None], wanted.shape)
    requests = (
        jnp.zeros((device_count, capacity + 1), jnp.int32)
        .at[rows, target]
        .set(columns)[:, :capacity]
    )
    source = keys_values.reshape(local_count, 2, cube, heads, head_size)
    padded = padded_2(keys_values, (("tm", 0), ("height", 1)), 1)
    padded = jnp.pad(padded, ((0, 0), (0, 0), (1, 1), (0, 0), (0, 0), (0, 0)))
    asked = lax.all_to_all(requests, ("tm", "height"), split_axis=0, concat_axis=0, tiled=True)
    tiles = lax.all_to_all(
        source[asked // heads, :, :, asked % heads, :],
        ("tm", "height"),
        split_axis=0,
        concat_axis=0,
        tiled=True,
    )
    received = tiles.reshape(device_count * capacity, 2, cube, head_size)
    first_time = lax.axis_index("tm") * span_time
    first_height = lax.axis_index("height") * span_height
    offsets = jnp.arange(3, dtype=jnp.int32) - 1
    scale = 1.0 / math.sqrt(head_size)
    zero = jnp.zeros((), jnp.int32)
    flat_queries = queries.reshape(local_count, cube, heads, head_size)

    def one_cube(index):
        time_pos = index // (span_height * span_width)
        height_pos = index // span_width % span_height
        width_pos = index % span_width
        window = lax.dynamic_slice(
            padded, (time_pos, height_pos, width_pos, zero, zero, zero), (3, 3, 3, 2, cube, width)
        )
        window = window.reshape(27, 2, cube, heads, head_size)
        global_time = first_time + time_pos + offsets
        global_height = first_height + height_pos + offsets
        global_width = width_pos + offsets
        inside_time = (global_time >= 0) & (global_time < grid_time)
        inside_height = (global_height >= 0) & (global_height < grid_height)
        inside_width = (global_width >= 0) & (global_width < span_width)
        valid = (
            inside_time[:, None, None] & inside_height[None, :, None] & inside_width[None, None, :]
        ).reshape(27)
        keys_window = window[:, 0].reshape(27 * cube, heads, head_size)
        values_window = window[:, 1].reshape(27 * cube, heads, head_size)
        far_tiles = received[far_slot[index]]
        query = flat_queries[index]
        score_window = (
            jnp.einsum("qhd,khd->hqk", query, keys_window, preferred_element_type=jnp.float32)
            * scale
        )
        score_window = jnp.where(jnp.repeat(valid, cube)[None, None, :], score_window, -jnp.inf)
        score_far = (
            jnp.einsum(
                "qhd,hfkd->hqfk", query, far_tiles[:, :, 0], preferred_element_type=jnp.float32
            )
            * scale
        )
        scores = jnp.concatenate(
            [score_window, score_far.reshape(heads, cube, far_count * cube)], axis=-1
        )
        largest = jnp.max(scores, axis=-1, keepdims=True)
        lifted = jnp.exp(scores - largest)
        weights = (lifted / jnp.sum(lifted, axis=-1, keepdims=True)).astype(jnp.bfloat16)
        attended = jnp.einsum(
            "hqk,khd->qhd",
            weights[:, :, : 27 * cube],
            values_window,
            preferred_element_type=jnp.float32,
        )
        far_weights = weights[:, :, 27 * cube :].reshape(heads, cube, far_count, cube)
        attended = attended + jnp.einsum(
            "hqfk,hfkd->qhd", far_weights, far_tiles[:, :, 1], preferred_element_type=jnp.float32
        )
        return attended.reshape(cube, width).astype(jnp.bfloat16)

    attended = lax.map(one_cube, jnp.arange(local_count, dtype=jnp.int32))
    output = jnp.dot(
        attended.reshape(local_count * cube, width), out_weight, preferred_element_type=jnp.float32
    )
    return output.astype(jnp.bfloat16).reshape(queries.shape)


def solution(mesh):
    in_specs = (
        P("tm", "height", None, None, None),
        P("tm", "height", None, None, None, None),
        P("tm", "height", None, None, None),
        P(),
    )
    out_specs = P("tm", "height", None, None, None)
    return jax.shard_map(body, mesh=mesh, in_specs=in_specs, out_specs=out_specs, check_vma=False)
```

profile of v0, /device:TPU:21, one launch (start us, length us, event | category | flops | bytes accessed | tf_op | source)
XLA Modules:
  0.0 875.0 jit_solution(9419864299019712610)
XLA Ops:
  1.0 37.5 %scatter_fusion = s32[32,48]{1,0:T(8,128)S(1)} fusion(s32[32,48]{1,0:T(8,128)S(1)} %broadcast.592, s32[768]{0:T(1024)S(1)} %reshape.498, s32[768]{0:T(1024)S(1)} %broadcast.656), kind=kCustom, calls=%fused_computation.3 | custom fusion | flops 768 | bytes 15360 | tf_op jit(solution)/shard_map/scatter-max | solution.py:47
  46.0 6.2 all-to-all-start
  56.2 10.9 %gather_fusion.2 = bf16[512,2,64,128]{3,2,1,0:T(8,128)(2,1)} fusion(bf16[2,2,64,24,128]{4,2,3,1,0:T(8,128)(2,1)S(1)} %copy.52, s32[512]{0:T(512)S(1)} %reshape.492), kind=kCustom, calls=%fused_computation.2 | custom fusion | bytes 33558528 | tf_op jit(solution)/shard_map/gather | solution.py:66
  67.1 7.2 all-to-all-start.1
  96.2 458.1 %collective-permute-done.2 = bf16[3,1,2,2,64,3072]{5,4,3,2,1,0:T(8,128)(2,1)} collective-permute-done((bf16[3,1,2,2,64,3072]{5,4,3,2,1,0:T(8,128)(2,1)}, bf16[3,1,2,2,64,3072]{5,4,3,2,1,0:T(8,128)(2,1)}, u32[]{:S(2)}, u32[]{:S(2)}) %collective-permute-start.2) | collective-permute-done | bytes 4718624 | tf_op jit(solution)/shard_map/ppermute | solution.py:19
  554.3 13.6 %fusion.33 = bf16[3,3,4,2,64,3072]{5,4,3,2,1,0:T(8,128)(2,1)} fusion(bf16[3,1,2,2,64,3072]{5,4,3,2,1,0:T(8,128)(2,1)} %collective-permute-done.3, bf16[3,1,2,2,64,3072]{5,4,3,2,1,0:T(8,128)(2,1)} %constant_dynamic-update-slice_fusion.1, bf16[3,1,2,2,64,3072]{5,4,3,2,1,0:T(8,128)(2,1)} %collective-permute-done.2), kind=kLoop, calls=%fused_computation.48 | loop fusion | flops 169869312 | bytes 42467328 | tf_op jit(solution)/shard_map/concatenate | solution.py:21
  568.0 296.9 %while.14 = (s32[]{:T(128)}, bf16[2,64,3072]{2,1,0:T(8,128)(2,1)}, s32[2]{0:T(128)S(1)}, bf16[3,3,4,2,64,3072]{5,4,3,2,1,0:T(8,128)(2,1)}, s32[]{:T(128)}, /*ind...) while((s32[]{:T(128)}, bf16[2,64,3072]{2,1,0:T(8,128)(2,1)}, ...), condition=%wide.region_7.8_spmd.clone.clone, body=%wide.region_3.7_spmd.clone.clone.sunk | while | flops 2205351168 | bytes 497691072 | solution.py:130
  570.7 15.1 %constant_dynamic-slice_fusion.5 = bf16[3,3,3,2,64,3072]{5,4,3,2,1,0:T(8,128)(2,1)} fusion(bf16[3,3,4,2,64,3072]{5,4,3,2,1,0:T(8,128)(2,1)} %get-tuple-element.345, s32[]{:T(128)S(6)} %select_n.356), kind=kLoop, calls=%fused_computation.35.clone.1 | loop fusion | bytes 42467332 | tf_op jit(solution)/shard_map/while/body/eval_jaxpr/dynamic_slice | solution.py:84
  585.8 12.1 %copy.91 = bf16[432,8,24,128]{3,2,1,0:T(8,128)(2,1)S(1)} copy(bf16[432,8,24,128]{3,1,2,0:T(8,128)(2,1)} %bitcast.178) | data formatting | bytes 42467328 | tf_op jit(solution)/shard_map/while
  597.9 7.0 fusion.89
  605.0 6.3 copy.92
  614.7 11.7 %fusion.90 = (f32[24,64]{1,0:T(8,128)S(1)}, f32[24,64,1728]{2,1,0:T(8,128)}) fusion(bf16[1728,24,128]{2,0,1:T(8,128)(2,1)} %bitcast.182, bf16[1,64,24,128]{3,2,1,0:T(8,128)(2,1)S(1)} %constant_dynamic-slice_fusion.4, pred[1728]{0:T(1024)(128)(4,1)S(1)} %broadcast_in_dim.91), kind=kOutput, calls=%fused_computation.132.clone.1 | convolution fusion | flops 687438336 | bytes 21634752 | tf_op jit(solution)/shard_map/while/body/eval_jaxpr/qhd,khd->hqk/dot_general | solution.py:102
  626.5 17.1 %gather_fusion = bf16[384,2,64,128]{3,2,1,0:T(8,128)(2,1)} fusion(bf16[512,2,64,128]{3,2,1,0:T(8,128)(2,1)} %get-tuple-element.350, s32[1024]{0:T(1024)S(1)} %pad_clamp_fusion.2), kind=kCustom, calls=%fused_computation.clone.clone.1 | custom fusion | bytes 25167360 | tf_op jit(solution)/shard_map/while/body/eval_jaxpr/gather | solution.py:99
  643.5 6.3 copy.89
  659.9 9.7 %copy.90 = f32[24,64,1024]{2,1,0:T(8,128)} copy(f32[24,64,1024]{1,2,0:T(8,128)} %bitcast.181) | data formatting | bytes 12582912 | tf_op jit(solution)/shard_map/while/body/eval_jaxpr/reshape | solution.py:113
  669.6 9.1 %fusion.91 = f32[24,64]{1,0:T(8,128)S(1)} fusion(f32[24,64,1024]{2,1,0:T(8,128)} %copy.90, f32[24,64,1728]{2,1,0:T(8,128)} %get-tuple-element.310, f32[24,64]{1,0:T(8,128)S(1)} %reduce_max.36), kind=kLoop, calls=%fused_computation.9.clone.1 | loop fusion | flops 12679680 | bytes 16920576 | tf_op jit(solution)/shard_map/while/body/eval_jaxpr/reduce_sum | solution.py:117
  678.8 7.9 divide_convert_fusion.2
  697.9 7.3 fusion.92
  705.3 7.6 copy.93
  719.1 15.1 %constant_dynamic-slice_fusion.5 = bf16[3,3,3,2,64,3072]{5,4,3,2,1,0:T(8,128)(2,1)} fusion(bf16[3,3,4,2,64,3072]{5,4,3,2,1,0:T(8,128)(2,1)} %get-tuple-element.345, s32[]{:T(128)S(6)} %select_n.356), kind=kLoop, calls=%fused_computation.35.clone.1 | loop fusion | bytes 42467332 | tf_op jit(solution)/shard_map/while/body/eval_jaxpr/dynamic_slice | solution.py:84
  734.2 12.1 %copy.91 = bf16[432,8,24,128]{3,2,1,0:T(8,128)(2,1)S(1)} copy(bf16[432,8,24,128]{3,1,2,0:T(8,128)(2,1)} %bitcast.178) | data formatting | bytes 42467328 | tf_op jit(solution)/shard_map/while
  746.3 7.0 fusion.89
  753.3 6.3 copy.92
  763.0 11.7 %fusion.90 = (f32[24,64]{1,0:T(8,128)S(1)}, f32[24,64,1728]{2,1,0:T(8,128)}) fusion(bf16[1728,24,128]{2,0,1:T(8,128)(2,1)} %bitcast.182, bf16[1,64,24,128]{3,2,1,0:T(8,128)(2,1)S(1)} %constant_dynamic-slice_fusion.4, pred[1728]{0:T(1024)(128)(4,1)S(1)} %broadcast_in_dim.91), kind=kOutput, calls=%fused_computation.132.clone.1 | convolution fusion | flops 687438336 | bytes 21634752 | tf_op jit(solution)/shard_map/while/body/eval_jaxpr/qhd,khd->hqk/dot_general | solution.py:102
  774.8 17.1 %gather_fusion = bf16[384,2,64,128]{3,2,1,0:T(8,128)(2,1)} fusion(bf16[512,2,64,128]{3,2,1,0:T(8,128)(2,1)} %get-tuple-element.350, s32[1024]{0:T(1024)S(1)} %pad_clamp_fusion.2), kind=kCustom, calls=%fused_computation.clone.clone.1 | custom fusion | bytes 25167360 | tf_op jit(solution)/shard_map/while/body/eval_jaxpr/gather | solution.py:99
  791.9 6.3 copy.89
  808.2 9.7 %copy.90 = f32[24,64,1024]{2,1,0:T(8,128)} copy(f32[24,64,1024]{1,2,0:T(8,128)} %bitcast.181) | data formatting | bytes 12582912 | tf_op jit(solution)/shard_map/while/body/eval_jaxpr/reshape | solution.py:113
  818.0 9.1 %fusion.91 = f32[24,64]{1,0:T(8,128)S(1)} fusion(f32[24,64,1024]{2,1,0:T(8,128)} %copy.90, f32[24,64,1728]{2,1,0:T(8,128)} %get-tuple-element.310, f32[24,64]{1,0:T(8,128)S(1)} %reduce_max.36), kind=kLoop, calls=%fused_computation.9.clone.1 | loop fusion | flops 12679680 | bytes 16920576 | tf_op jit(solution)/shard_map/while/body/eval_jaxpr/reduce_sum | solution.py:117
  827.1 7.9 divide_convert_fusion.2
  846.3 7.3 fusion.92
  853.6 7.6 copy.93
  864.9 10.1 %convolution_convert_fusion = bf16[128,3072]{1,0:T(8,128)(2,1)} fusion(bf16[128,3072]{1,0:T(8,128)(2,1)} %bitcast.188, bf16[3072,3072]{1,0:T(8,128)(2,1)} %param.9), kind=kOutput, calls=%fused_computation.49 | convolution fusion | flops 2416312320 | bytes 20447232 | tf_op jit(solution)/shard_map/dot_general | solution.py:131
  (129 shorter events, 88.1 us)
Async XLA Ops:
  0.9 37.8 %copy-start.9 = (s32[2]{0:T(128)S(1)}, s32[2]{0:T(128)}, u32[]{:S(2)}) copy-start(s32[2]{0:T(128)} %constant.246) | copy-start | bytes 28
  0.9 37.9 %copy-start.8 = (s32[2]{0:T(128)S(1)}, s32[2]{0:T(128)}, u32[]{:S(2)}) copy-start(s32[2]{0:T(128)} %constant.249) | copy-start | bytes 28
  1.0 51.3 %copy-start.3 = (bf16[1,1,2,2,64,3072]{5,4,3,2,1,0:T(8,128)(2,1)S(1)}, bf16[1,1,2,2,64,3072]{5,4,3,2,1,0:T(8,128)(2,1)}, u32[]{:S(2)}) copy-start(bf16[1,1,2,2,64,3072]{5,4,3,2,1,0:T(8,128)(2,1)} %param.7) | copy-start | bytes 4718596
  46.0 10.0 %all-to-all-start = ((s32[32,1,16]{2,1,0:T(1,128)}), s32[32,1,16]{2,1,0:T(1,128)S(1)}, u32[]{:S(2)}, u32[]{:S(2)}) async-start(s32[32,1,16]{2,1,0:T(1,128)} %copy.47), calls=%async_computation | async-start | bytes 32768 | tf_op jit(solution)/shard_map/all_to_all | solution.py:64
  67.1 22.5 %copy-start.7 = (s32[1,1,2,24,16]{3,4,2,1,0:T(8,128)S(1)}, s32[1,1,2,24,16]{3,4,2,1,0:T(8,128)}, u32[]{:S(2)}) copy-start(s32[1,1,2,24,16]{3,4,2,1,0:T(8,128)} %param.8) | copy-start | bytes 9220
  67.1 500.8 %all-to-all-start.1 = ((bf16[32,16,2,64,128]{4,3,2,1,0:T(8,128)(2,1)}), bf16[32,16,2,64,128]{4,3,2,1,0:T(8,128)(2,1)}, u32[]{:S(2)}, u32[]{:S(2)}) async-start(bf16[32,16,2,64,128]{4,3,2,1,0:T(8,128)(2,1)} %bitcast.185), calls=%async_computation.1 | async-start | bytes 33554432 | tf_op jit(solution)/shard_map/all_to_all | solution.py:65
  74.4 5.3 collective-permute-start
  75.7 6.5 collective-permute-start.1
  83.5 470.9 %collective-permute-start.2 = (bf16[3,1,2,2,64,3072]{5,4,3,2,1,0:T(8,128)(2,1)}, bf16[3,1,2,2,64,3072]{5,4,3,2,1,0:T(8,128)(2,1)}, u32[]{:S(2)}, u32[]{:S(2)}) collective-permute-start(bf16[3,1,2,2,64,3072]{5,4,3,2,1,0:T(8,128)(2,1)} %constant_dynamic-update-slice_fusion.1), channel_id=1, source_target_pairs={{0,1},{1,2},{2,3},{3,4},{4,5},{5,6},{6,7},{8,9},{9,10},{10,11},{11... | collective-permute-start | bytes 14155784 | tf_op jit(solution)/shard_map/ppermute | solution.py:19
  86.6 467.8 %collective-permute-start.3 = (bf16[3,1,2,2,64,3072]{5,4,3,2,1,0:T(8,128)(2,1)}, bf16[3,1,2,2,64,3072]{5,4,3,2,1,0:T(8,128)(2,1)}, u32[]{:S(2)}, u32[]{:S(2)}) collective-permute-start(bf16[3,1,2,2,64,3072]{5,4,3,2,1,0:T(8,128)(2,1)} %constant_dynamic-update-slice_fusion.1), channel_id=1, source_target_pairs={{1,0},{2,1},{3,2},{4,3},{5,4},{6,5},{7,6},{9,8},{10,9},{11,10},{12... | collective-permute-start | bytes 14155784 | tf_op jit(solution)/shard_map/ppermute | solution.py:20
  89.9 5.2 copy-start.6
  649.9 4.5 copy-start.2
  669.6 9.2 %copy-start = (f32[24,64,1024]{2,1,0:T(8,128)S(1)}, f32[24,64,1024]{2,1,0:T(8,128)}, u32[]{:S(2)}) copy-start(f32[24,64,1024]{2,1,0:T(8,128)} %copy.90) | copy-start | bytes 18874372 | tf_op jit(solution)/shard_map/while
  686.7 3.4 copy-start.1
  705.2 7.6 slice-start
  705.3 7.6 slice-start.1
  705.3 7.6 slice-start.2
  712.9 2.7 copy-start.4
  715.6 0.9 copy-start.5
  798.2 4.5 copy-start.2
  818.0 9.2 %copy-start = (f32[24,64,1024]{2,1,0:T(8,128)S(1)}, f32[24,64,1024]{2,1,0:T(8,128)}, u32[]{:S(2)}) copy-start(f32[24,64,1024]{2,1,0:T(8,128)} %copy.90) | copy-start | bytes 18874372 | tf_op jit(solution)/shard_map/while
  835.1 3.4 copy-start.1
  853.6 7.6 slice-start
  853.6 7.6 slice-start.1
  853.6 7.6 slice-start.2
  861.2 2.7 copy-start.4
  864.0 0.9 copy-start.5
where the time goes:
time: 876 us; the launch traced here: 875 us
  waiting for transfers between devices  462 us (53%)
  local copies, waits for them, and re-layouts  230 us (26%)
  other arithmetic  86.9 us (10%)
  matrix products  63.6 us (7%)
  starting transfers between devices  24 us (3%)
    ppermute x2, waiting for transfers between devices, padded_2(): before = lax.ppermute(last, axis, up)  459 us
    gather x4, local copies, waits for them, and re-layouts, one_cube(): far_tiles = received[far_slot[index]]  46.8 us
    while x34, local copies, waits for them, and re-layouts  41.9 us
    another operation x1, other arithmetic, body(): jnp.zeros((device_count, local_count * heads), jnp.int32)  37.5 us
    dynamic_slice x2, local copies, waits for them, and re-layouts, one_cube(): lax.dynamic_slice(padded, (time_pos, height_pos, width_pos, zero, zero, z...  30.3 us
    slice x4, local copies, waits for them, and re-layouts, one_cube(): values_window = window[:, 1].reshape(27 * cube, heads, head_size)  29.2 us
    dot_general x2, matrix products, one_cube(): jnp.einsum('qhd,khd->hqk', query, keys_window, preferred_element_type=jnp...  23.4 us
    reshape x2, local copies, waits for them, and re-layouts, one_cube(): score_far.reshape(heads, cube, far_count * cube)  19.5 us
  transfers between devices with their start and end apart: 6, of which 3 were waited for; matrix products, arithmetic and copies ran while one was open for 3% of the time, Pallas kernels for 0%

commit v1 on v0

--- a/solution.py
+++ b/solution.py
@@ -1,12 +1,17 @@
+import functools
 import math
 
 import jax
 import jax.numpy as jnp
 from jax import lax
+from jax.experimental import pallas as pl
+from jax.experimental.pallas import tpu as pltpu
 from jax.sharding import PartitionSpec as P
 
 HEADS = 24
 SLOTS = 512
+HEAD_DIM = 128
+LOG2E = math.log2(math.e)
 
 
 def padded_2(shard, sides, width):
@@ -134,6 +139,219 @@
     return output.astype(jnp.bfloat16).reshape(queries.shape)
 
 
+def prepare_kernel(q_ref, kv_ref, far_ref, small_ref, large_ref):
+    groups = q_ref.shape[2] // (3 * HEAD_DIM)
+    cubes = lax.broadcasted_iota(jnp.int32, (1, HEAD_DIM), 1)
+    counts = jnp.zeros((far_ref.shape[0], HEAD_DIM), jnp.float32)
+    for f in range(far_ref.shape[1]):
+        counts += (far_ref[:, f : f + 1] == cubes).astype(jnp.float32)
+    first_row = lax.broadcasted_iota(jnp.int32, (16, HEAD_DIM), 0) == 0
+    heads = 3 * groups
+    for chip in range(2):
+        for core in range(2):
+            for g in range(groups):
+                to = (chip * 2 + core) * groups + g
+                whole = 3 * g + 2 * chip
+                shared = 3 * g + 1
+                lanes = slice(whole * HEAD_DIM, (whole + 1) * HEAD_DIM)
+                large_ref[to, 0:64, :] = q_ref[core, :, lanes]
+                large_ref[to, 64:128, :] = kv_ref[core, 0, :, lanes]
+                large_ref[to, 128:192, :] = kv_ref[core, 1, :, lanes]
+                lanes = slice(shared * HEAD_DIM, (shared + 1) * HEAD_DIM)
+                small_ref[to, 0:64, :] = kv_ref[core, chip, :, lanes]
+                small_ref[to, 64:96, :] = q_ref[core, 32 * chip : 32 * chip + 32, lanes]
+                row = core * heads
+                small_ref[to, 96:112, :] = jnp.where(
+                    first_row,
+                    counts[row + whole : row + whole + 1],
+                    counts[row + shared : row + shared + 1],
+                ).astype(jnp.bfloat16)
+
+
+def attend(q_at, counts_ref, keys_ref, values_ref, out_ref, bias_ref, height_count, row):
+    sources, tokens = out_ref.shape[:2]
+    per_block = 256 // tokens
+    keys = keys_ref.shape[0]
+    key_cubes = keys // 64
+    chunk = 512
+    listed = counts_ref[:, 96 + row, :].astype(jnp.float32)
+    source = lax.broadcasted_iota(jnp.int32, listed.shape, 0)
+    cube = lax.broadcasted_iota(jnp.int32, listed.shape, 1)
+    other = cube // 2
+    near = (jnp.abs(source // height_count - other // height_count) <= 1) & (
+        jnp.abs(source % height_count - other % height_count) <= 1
+    )
+    counts = (listed + jnp.where(near & (cube < key_cubes), 1.0, 0.0)).astype(jnp.bfloat16)
+    for start in range(0, keys, chunk):
+        spread = (
+            lax.broadcasted_iota(jnp.int32, (HEAD_DIM, chunk), 0)
+            == (lax.broadcasted_iota(jnp.int32, (HEAD_DIM, chunk), 1) + start) // 64
+        ).astype(jnp.bfloat16)
+        wide = jnp.dot(counts, spread, preferred_element_type=jnp.float32)
+        bias_ref[:, start : start + chunk] = jnp.where(wide < 0.5, -1e30, jnp.where(wide > 1.5, 1.0, 0.0))
+    scale = LOG2E / math.sqrt(HEAD_DIM)
+
+    def block(index, carry):
+        first = index * per_block
+        query = q_at(first, per_block)
+        scores = []
+        top = None
+        for start in range(0, keys, chunk):
+            raw = lax.dot_general(
+                query,
+                keys_ref[start : start + chunk, :],
+                (((1,), (1,)), ((), ())),
+                preferred_element_type=jnp.float32,
+            )
+            rows = [
+                raw[i * tokens : (i + 1) * tokens] * scale
+                + bias_ref[pl.ds(first + i, 1), start : start + chunk]
+                for i in range(per_block)
+            ]
+            part = jnp.concatenate(rows, axis=0)
+            scores.append(part)
+            for lane in range(0, chunk, HEAD_DIM):
+                piece = part[:, lane : lane + HEAD_DIM]
+                top = piece if top is None else jnp.maximum(top, piece)
+        largest = jnp.max(top, axis=1, keepdims=True)
+        total = jnp.zeros((256, HEAD_DIM), jnp.float32)
+        mixed = jnp.zeros((256, HEAD_DIM), jnp.float32)
+        for n, start in enumerate(range(0, keys, chunk)):
+            lifted = jnp.exp2(scores[n] - largest)
+            for lane in range(0, chunk, HEAD_DIM):
+                total += lifted[:, lane : lane + HEAD_DIM]
+            mixed += jnp.dot(
+                lifted.astype(jnp.bfloat16),
+                values_ref[start : start + chunk, :],
+                preferred_element_type=jnp.float32,
+            )
+        result = mixed / jnp.sum(total, axis=1, keepdims=True)
+        out_ref[pl.ds(first, per_block)] = result.astype(jnp.bfloat16).reshape(
+            per_block, tokens, HEAD_DIM
+        )
+        return carry
+
+    lax.fori_loop(0, sources // per_block, block, 0)
+
+
+def large_kernel(height_count, mine_ref, other_ref, counts_ref, out_ref, keys_ref, values_ref, bias_ref):
+    core = lax.axis_index("tm") % 2
+    for s in range(mine_ref.shape[0]):
+        here = pl.multiple_of(s * 128 + core * 64, 64)
+        there = pl.multiple_of(s * 128 + (1 - core) * 64, 64)
+        keys_ref[pl.ds(here, 64), :] = mine_ref[s, 64:128, :]
+        values_ref[pl.ds(here, 64), :] = mine_ref[s, 128:192, :]
+        keys_ref[pl.ds(there, 64), :] = other_ref[s, 0:64, :]
+        values_ref[pl.ds(there, 64), :] = other_ref[s, 64:128, :]
+
+    def q_at(first, count):
+        return mine_ref[pl.ds(first, count), 0:64, :].reshape(count * 64, HEAD_DIM)
+
+    attend(q_at, counts_ref, keys_ref, values_ref, out_ref, bias_ref, height_count, 0)
+
+
+def small_kernel(
+    height_count, mine_ref, chip_ref, core_mine_ref, core_chip_ref, out_ref, keys_ref, values_ref, bias_ref
+):
+    core = lax.axis_index("tm") % 2
+    chip = lax.axis_index("tm") // 2
+
+    def fill(first_ref, second_ref, core_first_ref, core_second_ref):
+        for s in range(mine_ref.shape[0]):
+            here = pl.multiple_of(s * 128 + core * 64, 64)
+            there = pl.multiple_of(s * 128 + (1 - core) * 64, 64)
+            keys_ref[pl.ds(here, 64), :] = first_ref[s, 0:64, :]
+            values_ref[pl.ds(here, 64), :] = second_ref[s, 0:64, :]
+            keys_ref[pl.ds(there, 64), :] = core_first_ref[s]
+            values_ref[pl.ds(there, 64), :] = core_second_ref[s]
+
+    @pl.when(chip == 0)
+    def _():
+        fill(mine_ref, chip_ref, core_mine_ref, core_chip_ref)
+
+    @pl.when(chip == 1)
+    def _():
+        fill(chip_ref, mine_ref, core_chip_ref, core_mine_ref)
+
+    def q_at(first, count):
+        return mine_ref[pl.ds(first, count), 64:96, :].reshape(count * 32, HEAD_DIM)
+
+    attend(q_at, mine_ref, keys_ref, values_ref, out_ref, bias_ref, height_count, 1)
+
+
+def by_heads(queries, keys_values, far_cubes, out_weight):
+    tm_count = lax.axis_size("tm")
+    height_count = lax.axis_size("height")
+    devices = tm_count * height_count
+    width = queries.shape[-1]
+    heads = width // HEAD_DIM
+    axes = ("tm", "height")
+    bf16 = jnp.bfloat16
+    params = pltpu.CompilerParams(vmem_limit_bytes=56 * 2**20)
+    small, large = pl.pallas_call(
+        prepare_kernel,
+        out_shape=(
+            jax.ShapeDtypeStruct((devices, 112, HEAD_DIM), bf16),
+            jax.ShapeDtypeStruct((devices, 192, HEAD_DIM), bf16),
+        ),
+        compiler_params=params,
+        name="prepare",
+    )(
+        queries.reshape(2, 64, width),
+        keys_values.reshape(2, 2, 64, width),
+        far_cubes.reshape(2 * heads, far_cubes.shape[-1]),
+    )
+    other_core = [(i, i ^ 1) for i in range(tm_count)]
+    other_chip = [(i, i ^ 2) for i in range(tm_count)]
+    scratch = [
+        pltpu.VMEM((devices * 128, HEAD_DIM), bf16),
+        pltpu.VMEM((devices * 128, HEAD_DIM), bf16),
+        pltpu.VMEM((devices, devices * 128), jnp.float32),
+    ]
+
+    def cost(tokens):
+        work = devices * tokens * devices * 128
+        return pl.CostEstimate(
+            flops=4 * work * HEAD_DIM, bytes_accessed=8 * 2**20, transcendentals=work
+        )
+
+    got_small = lax.all_to_all(small, axes, 0, 0, tiled=True)
+    mine = got_small[:, :64]
+    chip = lax.ppermute(mine, "tm", other_chip)
+    core_mine = lax.ppermute(mine, "tm", other_core)
+    core_chip = lax.ppermute(chip, "tm", other_core)
+    out_small = pl.pallas_call(
+        functools.partial(small_kernel, height_count),
+        out_shape=jax.ShapeDtypeStruct((devices, 32, HEAD_DIM), bf16),
+        scratch_shapes=scratch,
+        compiler_params=params,
+        cost_estimate=cost(32),
+        name="attend_small",
+    )(got_small, chip, core_mine, core_chip)
+
+    got_large = lax.all_to_all(large, axes, 0, 0, tiled=True)
+    core_large = lax.ppermute(got_large[:, 64:], "tm", other_core)
+    out_large = pl.pallas_call(
+        functools.partial(large_kernel, height_count),
+        out_shape=jax.ShapeDtypeStruct((devices, 64, HEAD_DIM), bf16),
+        scratch_shapes=scratch,
+        compiler_params=params,
+        cost_estimate=cost(64),
+        name="attend_large",
+    )(got_large, core_large, got_small)
+
+    back_small = lax.all_to_all(out_small, axes, 0, 0, tiled=True)
+    back_large = lax.all_to_all(out_large, axes, 0, 0, tiled=True)
+    back_small = back_small.reshape(2, 2, height_count, 32, HEAD_DIM).transpose(1, 0, 3, 2, 4)
+    back_small = back_small.reshape(2, 64, height_count, 1, HEAD_DIM)
+    back_large = back_large.reshape(2, 2, height_count, 64, HEAD_DIM).transpose(1, 3, 2, 0, 4)
+    attended = jnp.concatenate([back_large[:, :, :, :1], back_small, back_large[:, :, :, 1:]], axis=3)
+    output = jnp.dot(
+        attended.reshape(128, width), out_weight, preferred_element_type=jnp.float32
+    )
+    return output.astype(bf16).reshape(queries.shape)
+
+
 def solution(mesh):
     in_specs = (
         P("tm", "height", None, None, None),
@@ -142,4 +360,5 @@
         P(),
     )
     out_specs = P("tm", "height", None, None, None)
-    return jax.shard_map(body, mesh=mesh, in_specs=in_specs, out_specs=out_specs, check_vma=False)
+    fits = mesh.shape["tm"] == 4 and HEADS == 3 * mesh.shape["height"]
+    return jax.shard_map(by_heads if fits else body, mesh=mesh, in_specs=in_specs, out_specs=out_specs, check_vma=False)

time: 876 us -> 150 us (0.17)
  the two profiles are of different devices: /device:TPU:21 before, /device:TPU:0 now
where the time goes in v1:
time: 150 us
  waiting for transfers between devices  56.3 us (38%)
  Pallas kernels  32.6 us (22%)
  blocking collectives  32.1 us (21%)
  starting transfers between devices  13.4 us (9%)
  matrix products  9.86 us (7%)
  local copies, waits for them, and re-layouts  5.46 us (4%)
    all_to_all x1, waiting for transfers between devices, by_heads(): got_large = lax.all_to_all(large, axes, 0, 0, tiled=True)  36.3 us
    all_to_all x1, blocking collectives, by_heads(): got_small = lax.all_to_all(small, axes, 0, 0, tiled=True)  32.1 us
    pallas_call x1, Pallas kernels, by_heads(): pl.pallas_call(functools.partial(large_kernel, height_count), out_shape=j...  18.7 us
    all_to_all x1, waiting for transfers between devices, by_heads(): back_large = lax.all_to_all(out_large, axes, 0, 0, tiled=True)  16.2 us
    pallas_call x1, Pallas kernels, by_heads(): pl.pallas_call(functools.partial(small_kernel, height_count), out_shape=j...  10.6 us
    dot_general x1, matrix products, by_heads(): jnp.dot(attended.reshape(128, width), out_weight, preferred_element_type=...  9.86 us
    all_to_all x1, starting transfers between devices, by_heads(): back_large = lax.all_to_all(out_large, axes, 0, 0, tiled=True)  5.83 us
    pallas_call x1, Pallas kernels, by_heads(): pl.pallas_call(prepare_kernel, out_shape=(jax.ShapeDtypeStruct((devices,...  3.31 us
  transfers between devices with their start and end apart: 7, of which 4 were waited for; matrix products, arithmetic and copies ran while one was open for 1% of the time, Pallas kernels for 20%

profile of v1, /device:TPU:0, one launch (start us, length us, event | category | flops | bytes accessed | tf_op | source)
XLA Modules:
  0.0 149.9 jit_solution(14952012013207900025)
XLA Ops:
  0.0 1.4 copy.6
  1.4 3.3 %prepare.1 = (bf16[32,112,128]{2,1,0:T(8,128)(2,1)}, bf16[32,192,128]{2,1,0:T(8,128)(2,1)}) custom-call(bf16[2,64,3072]{2,1,0:T(8,128)(2,1)} %bitcast.19, bf16[2,2,64,3072]{3,2,1,0:T(8,128)(2,1)} %bitcast.16, s32[48,16]{1,0:T(8,128)} %bitcast.20), custom_call_target="tpu_custom_call" | custom-call | tf_op jit(solution)/shard_map/prepare/pallas_call | solution.py:291
  4.7 32.1 %all_to_all.20.counts_ref.mine_ref = bf16[32,112,128]{2,1,0:T(8,128)(2,1)S(1)} all-to-all(bf16[32,112,128]{2,1,0:T(8,128)(2,1)} %get-tuple-element.8), channel_id=1, replica_groups=mesh['tm'=4,'height'=8] {'tm','height'}, dimensions={0} | all-to-all | bytes 1835008 | tf_op jit(solution)/shard_map/all_to_all | solution.py:318
  36.8 2.7 %all-to-all-start = ((bf16[32,192,128]{2,1,0:T(8,128)(2,1)}), bf16[32,192,128]{2,1,0:T(8,128)(2,1)S(1)}, u32[]{:S(2)}, u32[]{:S(2)}) async-start(bf16[32,192,128]{2,1,0:T(8,128)(2,1)} %get-tuple-element.7), calls=%async_computation | async-start | bytes 3145728 | tf_op jit(solution)/shard_map/all_to_all | solution.py:332
  39.5 0.9 slice.18
  40.3 1.7 %collective-permute-start.1 = (bf16[32,64,128]{2,1,0:T(8,128)(2,1)}, bf16[32,64,128]{2,1,0:T(8,128)(2,1)}, u32[]{:S(2)}, u32[]{:S(2)}) collective-permute-start(bf16[32,64,128]{2,1,0:T(8,128)(2,1)} %slice.18), channel_id=1, source_target_pairs={{0,16},{8,24},{16,0},{24,8},{1,17},{9,25},{17,1},{25,9},{2,18},{10... | collective-permute-start | bytes 1572872 | tf_op jit(solution)/shard_map/ppermute | solution.py:320
  42.0 36.3 %all-to-all-done.mine_ref = bf16[32,192,128]{2,1,0:T(8,128)(2,1)S(1)} async-done(((bf16[32,192,128]{2,1,0:T(8,128)(2,1)}), bf16[32,192,128]{2,1,0:T(8,128)(2,1)S(1)}, u32[]{:S(2)}, u32[]{:S(2)}) %all-to-all-start) | async-done | bytes 1572896 | tf_op jit(solution)/shard_map/all_to_all | solution.py:332
  78.3 0.0 copy-start
  78.3 0.1 slice.16
  78.4 0.1 collective-permute-start
  78.5 0.5 collective-permute-start.2
  79.0 0.0 collective-permute-done.1.chip_ref
  79.0 0.1 collective-permute-start.3
  79.1 3.0 %collective-permute-done.2.core_mine_ref = bf16[32,64,128]{2,1,0:T(8,128)(2,1)S(1)} collective-permute-done((bf16[32,64,128]{2,1,0:T(8,128)(2,1)}, bf16[32,64,128]{2,1,0:T(8,128)(2,1)S(1)}, u32[]{:S(2)}, u32[]{:S(2)}) %collective-permute-start.2) | collective-permute-done | bytes 524320 | tf_op jit(solution)/shard_map/ppermute | solution.py:321
  82.1 0.7 collective-permute-done.3.core_chip_ref
  82.8 0.0 copy-done.1
  82.8 0.0 copy-done.2
  82.9 0.8 copy-done.3
  83.7 10.6 %attend_small.1 = bf16[32,32,128]{2,1,0:T(8,128)(2,1)} custom-call(bf16[32,112,128]{2,1,0:T(8,128)(2,1)} %copy-done.1, bf16[32,64,128]{2,1,0:T(8,128)(2,1)} %collective-permute-done.1.chip_ref, bf16[32,64,128]{2,1,0:T(8,128)(2,1)} %copy-done.2, bf16[32,64,128]{2,1,0:T(8,128)(2,1)} %copy-done.3), custom_call_target="tpu_custom_call" | custom-call | flops 2147483648 | bytes 8388608 | tf_op jit(solution)/shard_map/attend_small/pallas_call | solution.py:323
  94.2 2.6 %all-to-all-start.3 = ((bf16[32,32,128]{2,1,0:T(8,128)(2,1)}), bf16[32,32,128]{2,1,0:T(8,128)(2,1)S(1)}, u32[]{:S(2)}, u32[]{:S(2)}) async-start(bf16[32,32,128]{2,1,0:T(8,128)(2,1)} %attend_small.1), calls=%async_computation.3 | async-start | bytes 524288 | tf_op jit(solution)/shard_map/all_to_all | solution.py:343
  96.8 0.0 collective-permute-done.other_ref
  96.8 0.0 copy-done
  96.9 18.7 %attend_large.1 = bf16[32,64,128]{2,1,0:T(8,128)(2,1)} custom-call(bf16[32,192,128]{2,1,0:T(8,128)(2,1)} %copy-done, bf16[32,128,128]{2,1,0:T(8,128)(2,1)} %collective-permute-done.other_ref, bf16[32,112,128]{2,1,0:T(8,128)(2,1)} %copy-done.1), custom_call_target="tpu_custom_call" | custom-call | flops 4294967296 | bytes 8388608 | tf_op jit(solution)/shard_map/attend_large/pallas_call | solution.py:334
  115.6 0.0 all-to-all-done.3
  115.6 5.8 %all-to-all-start.2 = ((bf16[32,64,128]{2,1,0:T(8,128)(2,1)}), bf16[32,64,128]{2,1,0:T(8,128)(2,1)S(1)}, u32[]{:S(2)}, u32[]{:S(2)}) async-start(bf16[32,64,128]{2,1,0:T(8,128)(2,1)} %attend_large.1), calls=%async_computation.2 | async-start | bytes 1048576 | tf_op jit(solution)/shard_map/all_to_all | solution.py:344
  121.4 0.1 copy.8
  121.5 16.2 %all-to-all-done.2 = bf16[32,64,128]{2,1,0:T(8,128)(2,1)S(1)} async-done(((bf16[32,64,128]{2,1,0:T(8,128)(2,1)}), bf16[32,64,128]{2,1,0:T(8,128)(2,1)S(1)}, u32[]{:S(2)}, u32[]{:S(2)}) %all-to-all-start.2) | async-done | bytes 524320 | tf_op jit(solution)/shard_map/all_to_all | solution.py:344
  137.7 0.3 copy.11
  138.1 0.1 pad_maximum_fusion
  138.2 1.1 copy.9
  139.3 0.7 reshape.30
  140.0 9.9 %convolution_convert_fusion = bf16[128,3072]{1,0:T(8,128)(2,1)} fusion(bf16[128,3072]{1,0:T(8,128)(2,1)S(1)} %reshape.30, bf16[3072,3072]{1,0:T(8,128)(2,1)} %param.7), kind=kOutput, calls=%fused_computation | convolution fusion | flops 2416312320 | bytes 20447232 | tf_op jit(solution)/shard_map/dot_general | solution.py:349
  (4 shorter events, 0.0 us)
Async XLA Ops:
  36.8 46.0 %copy-start.1 = (bf16[32,112,128]{2,1,0:T(8,128)(2,1)}, bf16[32,112,128]{2,1,0:T(8,128)(2,1)S(1)}, u32[]{:S(2)}) copy-start(bf16[32,112,128]{2,1,0:T(8,128)(2,1)S(1)} %all_to_all.20.counts_ref.mine_ref) | copy-start | bytes 2752516
  36.8 41.5 %all-to-all-start = ((bf16[32,192,128]{2,1,0:T(8,128)(2,1)}), bf16[32,192,128]{2,1,0:T(8,128)(2,1)S(1)}, u32[]{:S(2)}, u32[]{:S(2)}) async-start(bf16[32,192,128]{2,1,0:T(8,128)(2,1)} %get-tuple-element.7), calls=%async_computation | async-start | bytes 3145728 | tf_op jit(solution)/shard_map/all_to_all | solution.py:332
  40.3 38.6 %collective-permute-start.1 = (bf16[32,64,128]{2,1,0:T(8,128)(2,1)}, bf16[32,64,128]{2,1,0:T(8,128)(2,1)}, u32[]{:S(2)}, u32[]{:S(2)}) collective-permute-start(bf16[32,64,128]{2,1,0:T(8,128)(2,1)} %slice.18), channel_id=1, source_target_pairs={{0,16},{8,24},{16,0},{24,8},{1,17},{9,25},{17,1},{25,9},{2,18},{10... | collective-permute-start | bytes 1572872 | tf_op jit(solution)/shard_map/ppermute | solution.py:320
  78.3 18.5 %copy-start = (bf16[32,192,128]{2,1,0:T(8,128)(2,1)}, bf16[32,192,128]{2,1,0:T(8,128)(2,1)S(1)}, u32[]{:S(2)}) copy-start(bf16[32,192,128]{2,1,0:T(8,128)(2,1)S(1)} %all-to-all-done.mine_ref) | copy-start | bytes 4718596
  78.4 18.4 %collective-permute-start = (bf16[32,128,128]{2,1,0:T(8,128)(2,1)S(1)}, bf16[32,128,128]{2,1,0:T(8,128)(2,1)}, u32[]{:S(2)}, u32[]{:S(2)}) collective-permute-start(bf16[32,128,128]{2,1,0:T(8,128)(2,1)S(1)} %slice.16), channel_id=1, source_target_pairs={{0,8},{8,0},{16,24},{24,16},{1,9},{9,1},{17,25},{25,17},{2,10},{10... | collective-permute-start | bytes 3145736 | tf_op jit(solution)/shard_map/ppermute | solution.py:333
  78.5 3.6 %collective-permute-start.2 = (bf16[32,64,128]{2,1,0:T(8,128)(2,1)}, bf16[32,64,128]{2,1,0:T(8,128)(2,1)S(1)}, u32[]{:S(2)}, u32[]{:S(2)}) collective-permute-start(bf16[32,64,128]{2,1,0:T(8,128)(2,1)} %slice.18), channel_id=1, source_target_pairs={{0,8},{8,0},{16,24},{24,16},{1,9},{9,1},{17,25},{25,17},{2,10},{10... | collective-permute-start | bytes 1572872 | tf_op jit(solution)/shard_map/ppermute | solution.py:321
  79.0 3.9 %collective-permute-start.3 = (bf16[32,64,128]{2,1,0:T(8,128)(2,1)}, bf16[32,64,128]{2,1,0:T(8,128)(2,1)S(1)}, u32[]{:S(2)}, u32[]{:S(2)}) collective-permute-start(bf16[32,64,128]{2,1,0:T(8,128)(2,1)} %collective-permute-done.1.chip_ref), channel_id=1, source_target_pairs={{0,8},{8,0},{16,24},{24,16},{1,9},{9,1},{17,25},{25,17},{2,10},{10... | collective-permute-start | bytes 1572872 | tf_op jit(solution)/shard_map/ppermute | solution.py:322
  82.1 0.8 copy-start.2
  82.9 0.8 copy-start.3
  94.2 21.3 %all-to-all-start.3 = ((bf16[32,32,128]{2,1,0:T(8,128)(2,1)}), bf16[32,32,128]{2,1,0:T(8,128)(2,1)S(1)}, u32[]{:S(2)}, u32[]{:S(2)}) async-start(bf16[32,32,128]{2,1,0:T(8,128)(2,1)} %attend_small.1), calls=%async_computation.3 | async-start | bytes 524288 | tf_op jit(solution)/shard_map/all_to_all | solution.py:343
  115.6 22.2 %all-to-all-start.2 = ((bf16[32,64,128]{2,1,0:T(8,128)(2,1)}), bf16[32,64,128]{2,1,0:T(8,128)(2,1)S(1)}, u32[]{:S(2)}, u32[]{:S(2)}) async-start(bf16[32,64,128]{2,1,0:T(8,128)(2,1)} %attend_large.1), calls=%async_computation.2 | async-start | bytes 1048576 | tf_op jit(solution)/shard_map/all_to_all | solution.py:344

commit v2 on v0

--- a/solution.py
+++ b/solution.py
@@ -1,12 +1,25 @@
+import functools
 import math
 
 import jax
 import jax.numpy as jnp
+import ml_dtypes
+import numpy as np
 from jax import lax
+from jax.experimental import pallas as pl
+from jax.experimental.pallas import tpu as pltpu
 from jax.sharding import PartitionSpec as P
 
 HEADS = 24
 SLOTS = 512
+HEAD_DIM = 128
+LOG2E = math.log2(math.e)
+SCALE = LOG2E / math.sqrt(HEAD_DIM)
+TWICE = 1.0 / SCALE
+TWICE_HIGH = float(np.asarray(TWICE, ml_dtypes.bfloat16))
+TWICE_LOW = TWICE - TWICE_HIGH
+ROWS = 256
+CHUNK = 512
 
 
 def padded_2(shard, sides, width):
@@ -134,6 +147,414 @@
     return output.astype(jnp.bfloat16).reshape(queries.shape)
 
 
+def head_lanes(head):
+    return slice(head * HEAD_DIM, (head + 1) * HEAD_DIM)
+
+
+def prepare_first(q_ref, kv_ref, far_ref, out_ref, q_in, kv_in, staged, sems):
+    groups = out_ref.shape[2]
+    span = 3 * HEAD_DIM
+
+    def copies_in(g):
+        lanes = pl.ds(g * span, span)
+        return (
+            pltpu.make_async_copy(q_ref.at[:, :, lanes], q_in.at[g], sems.at[0, g]),
+            pltpu.make_async_copy(kv_ref.at[:, :, :, lanes], kv_in.at[g], sems.at[1, g]),
+        )
+
+    def copy_out(g):
+        return pltpu.make_async_copy(staged.at[:, :, g], out_ref.at[:, :, g], sems.at[2, g])
+
+    for g in range(groups):
+        for copy in copies_in(g):
+            copy.start()
+    cubes = lax.broadcasted_iota(jnp.int32, (far_ref.shape[1], HEAD_DIM), 1) % 64
+    top_row = lax.broadcasted_iota(jnp.int32, (8, HEAD_DIM), 0) == 0
+
+    def counts(core, head):
+        listed = far_ref[core, :, head : head + 1] == cubes
+        return jnp.sum(listed.astype(jnp.float32), axis=0, keepdims=True)
+
+    for g in range(groups):
+        for core in range(2):
+            shared = counts(core, 3 * g + 1)
+            for chip in range(2):
+                staged[chip, core, g, 256:264, :] = jnp.where(
+                    top_row, counts(core, 3 * g + 2 * chip), shared
+                ).astype(jnp.bfloat16)
+    for g in range(groups):
+        for copy in copies_in(g):
+            copy.wait()
+        for core in range(2):
+            for chip in range(2):
+                lanes = head_lanes(2 * chip)
+                staged[chip, core, g, 0:64, :] = q_in[g, core, :, lanes]
+                staged[chip, core, g, 64:128, :] = kv_in[g, core, 0, :, lanes]
+                staged[chip, core, g, 128:192, :] = kv_in[g, core, 1, :, lanes]
+                staged[chip, core, g, 192:256, :] = kv_in[g, core, chip, :, head_lanes(1)]
+        copy_out(g).start()
+    for g in range(groups):
+        copy_out(g).wait()
+
+
+def prepare_second(q_ref, out_ref, sems):
+    copies = []
+    for g in range(out_ref.shape[2]):
+        lanes = pl.ds((3 * g + 1) * HEAD_DIM, HEAD_DIM)
+        for chip in range(2):
+            copies.append(
+                pltpu.make_async_copy(
+                    q_ref.at[:, 32 * chip : 32 * chip + 32, lanes],
+                    out_ref.at[chip, :, g],
+                    sems.at[chip, g],
+                )
+            )
+    for copy in copies:
+        copy.start()
+    for copy in copies:
+        copy.wait()
+
+
+def set_constants(listed, bias_ref, height_count):
+    source = lax.broadcasted_iota(jnp.int32, listed.shape, 0)
+    lane = lax.broadcasted_iota(jnp.int32, listed.shape, 1)
+    place = lane % 64 // 2
+    near = (jnp.abs(source // height_count - place // height_count) <= 1) & (
+        jnp.abs(source % height_count - place % height_count) <= 1
+    )
+    counts = listed + jnp.where(near, 1.0, 0.0)
+    high = lane < 64
+    bias_ref[...] = jnp.where(
+        counts < 0.5,
+        jnp.where(high, -1e30, 0.0),
+        jnp.where(counts > 1.5, jnp.where(high, TWICE_HIGH, TWICE_LOW), 0.0),
+    )
+
+
+def set_margins(kv_ref):
+    shape = (2, 64, HEAD_DIM)
+    width = lax.broadcasted_iota(jnp.int32, shape, 0)
+    lane = lax.broadcasted_iota(jnp.int32, shape, 2) % 64
+    for s in range(kv_ref.shape[1]):
+        kv_ref[0, s, :, :, HEAD_DIM:] = (lane == 2 * s + width).astype(jnp.bfloat16)
+        kv_ref[1, s, :, :, HEAD_DIM:] = jnp.ones(shape, jnp.bfloat16)
+
+
+def attend(q_at, wait_values, kv_ref, bias_ref, out_ref, scores):
+    sources, tokens = out_ref.shape[:2]
+    step = ROWS // tokens
+    chunk = CHUNK // 128
+    chunks = range(0, sources, chunk)
+
+    def score(first, s_ref):
+        bias = [
+            jnp.broadcast_to(bias_ref[pl.ds(first + i, 1), :], (tokens, HEAD_DIM))
+            for i in range(step)
+        ]
+        bias = jnp.concatenate(bias, axis=0).astype(jnp.bfloat16)
+        query = jnp.concatenate([q_at(first, step), bias], axis=1)
+        top = None
+        for s in chunks:
+            part = lax.dot_general(
+                query,
+                kv_ref[0, s : s + chunk].reshape(CHUNK, 2 * HEAD_DIM),
+                (((1,), (1,)), ((), ())),
+                preferred_element_type=jnp.float32,
+            )
+            s_ref[:, s * 128 : s * 128 + CHUNK] = part
+            for lane in range(0, CHUNK, HEAD_DIM):
+                piece = part[:, lane : lane + HEAD_DIM]
+                top = piece if top is None else jnp.maximum(top, piece)
+        return jnp.max(top, axis=1, keepdims=True)
+
+    def mix(first, s_ref, largest):
+        mixed = jnp.zeros((ROWS, 2 * HEAD_DIM), jnp.float32)
+        for s in chunks:
+            lifted = jnp.exp2((s_ref[:, s * 128 : s * 128 + CHUNK] - largest) * SCALE)
+            mixed += jnp.dot(
+                lifted.astype(jnp.bfloat16),
+                kv_ref[1, s : s + chunk].reshape(CHUNK, 2 * HEAD_DIM),
+                preferred_element_type=jnp.float32,
+            )
+        result = (mixed[:, :HEAD_DIM] / mixed[:, HEAD_DIM:]).astype(out_ref.dtype)
+        out_ref[pl.ds(first, step)] = result.reshape(step, tokens, HEAD_DIM)
+
+    def two_blocks(index, largest):
+        first = index * 2 * step
+        later = score(first + step, scores[1])
+        mix(first, scores[0], largest)
+        following = jnp.minimum(first + 2 * step, sources - step)
+        largest = score(following, scores[0])
+        mix(first + step, scores[1], later)
+        return largest
+
+    largest = score(0, scores[0])
+    wait_values()
+    lax.fori_loop(0, sources // step // 2, two_blocks, largest)
+
+
+def pieces(count, source, target, sems, row):
+    part = count // 4
+    return [
+        pltpu.make_async_copy(
+            source(pl.ds(i * part, part)), target(pl.ds(i * part, part)), sems.at[row, i]
+        )
+        for i in range(4)
+    ]
+
+
+def large_kernel(
+    height_count, mine_ref, core_ref, info_in, out_ref, kv_ref, q_in, bias_ref, sems, *scores
+):
+    core = lax.axis_index("tm") % 2
+    count = mine_ref.shape[0]
+    own = [
+        pieces(
+            count,
+            lambda at, k=k: mine_ref.at[at, 64 + 64 * k : 128 + 64 * k, :],
+            lambda at, k=k: kv_ref.at[k, at, core, :, 0:HEAD_DIM],
+            sems,
+            k,
+        )
+        for k in range(2)
+    ]
+    other = [
+        pieces(
+            count,
+            lambda at, k=k: core_ref.at[at, 64 * k : 64 + 64 * k, :],
+            lambda at, k=k: kv_ref.at[k, at, 1 - core, :, 0:HEAD_DIM],
+            sems,
+            2 + k,
+        )
+        for k in range(2)
+    ]
+    query = pieces(count, lambda at: mine_ref.at[at, 0:64, :], lambda at: q_in.at[at], sems, 4)
+    for copy in own[0] + other[0] + query + own[1] + other[1]:
+        copy.start()
+    set_margins(kv_ref)
+    set_constants(info_in[:, 0, :].astype(jnp.float32), bias_ref, height_count)
+    for copy in own[0] + other[0] + query:
+        copy.wait()
+
+    def wait_values():
+        for copy in own[1] + other[1]:
+            copy.wait()
+
+    def q_at(first, count):
+        return q_in[pl.ds(first, count)].reshape(count * 64, HEAD_DIM)
+
+    attend(q_at, wait_values, kv_ref, bias_ref, out_ref, scores)
+
+
+def small_kernel(
+    height_count, first_ref, second_ref, chip_ref, core_mine_ref, core_chip_ref, info_in, out_ref,
+    kv_ref, q_in, bias_ref, sems, *scores
+):
+    core = lax.axis_index("tm") % 2
+    chip = lax.axis_index("tm") // 2
+    count = first_ref.shape[0]
+
+    def kept(source, kind, width, row):
+        return pieces(
+            count, source, lambda at: kv_ref.at[kind, at, width, :, 0:HEAD_DIM], sems, row
+        )
+
+    copies = pieces(count, lambda at: second_ref.at[at], lambda at: q_in.at[at], sems, 4)
+    copies += kept(lambda at: first_ref.at[at, 192:256, :], chip, core, 0)
+    copies += kept(lambda at: chip_ref.at[at], 1 - chip, core, 1)
+    copies += kept(lambda at: core_mine_ref.at[at], chip, 1 - core, 2)
+    copies += kept(lambda at: core_chip_ref.at[at], 1 - chip, 1 - core, 3)
+    for copy in copies:
+        copy.start()
+    set_margins(kv_ref)
+    set_constants(info_in[:, 1, :].astype(jnp.float32), bias_ref, height_count)
+    for copy in copies:
+        copy.wait()
+
+    def q_at(first, count):
+        return q_in[pl.ds(first, count)].reshape(count * 32, HEAD_DIM)
+
+    attend(q_at, lambda: None, kv_ref, bias_ref, out_ref, scores)
+
+
+def project_large(back_ref, weight_ref, part_ref, rest_ref, weights, sems):
+    groups = back_ref.shape[0] // 4
+
+    def copies(g):
+        return [
+            pltpu.make_async_copy(weight_ref.at[g, 2 * chip], weights.at[chip, g], sems.at[chip, g])
+            for chip in range(2)
+        ]
+
+    def rest(g):
+        return pltpu.make_async_copy(weight_ref.at[g, 1], rest_ref.at[g], sems.at[2, g])
+
+    for g in range(groups):
+        for copy in copies(g):
+            copy.start()
+    for g in range(groups):
+        rest(g).start()
+    total = None
+    for g in range(0, groups, 2):
+        for copy in copies(g) + copies(g + 1):
+            copy.wait()
+        for chip in range(2):
+            rows = [
+                jnp.concatenate(
+                    [back_ref[(chip * 2 + core) * groups + g + i] for i in range(2)], axis=1
+                )
+                for core in range(2)
+            ]
+            part = jnp.dot(
+                jnp.concatenate(rows, axis=0),
+                weights[chip, g : g + 2].reshape(2 * HEAD_DIM, weights.shape[-1]),
+                preferred_element_type=jnp.float32,
+            )
+            total = part if total is None else total + part
+    part_ref[...] = total
+    for g in range(groups):
+        rest(g).wait()
+
+
+def project_small(back_ref, weight_ref, part_ref, out_ref):
+    groups = back_ref.shape[0] // 4
+    rows = [
+        jnp.concatenate([back_ref[to * groups + g] for g in range(groups)], axis=1)
+        for to in (0, 2, 1, 3)
+    ]
+    attended = jnp.concatenate(rows, axis=0)
+    width = out_ref.shape[-1]
+    tile = width // 4
+    for start in range(0, width, tile):
+        weight = weight_ref[:, :, start : start + tile].reshape(groups * HEAD_DIM, tile)
+        total = part_ref[:, start : start + tile] + jnp.dot(
+            attended, weight, preferred_element_type=jnp.float32
+        )
+        out_ref[:, start : start + tile] = total.astype(out_ref.dtype)
+
+
+def by_heads(queries, keys_values, far_cubes, out_weight):
+    tm_count = lax.axis_size("tm")
+    height_count = lax.axis_size("height")
+    devices = tm_count * height_count
+    width = queries.shape[-1]
+    heads = width // HEAD_DIM
+    far_count = far_cubes.shape[-1]
+    axes = ("tm", "height")
+    bf16, f32 = jnp.bfloat16, jnp.float32
+    params = pltpu.CompilerParams(vmem_limit_bytes=60 * 2**20)
+    anywhere = pl.BlockSpec(memory_space=pl.ANY)
+    queries_in = queries.reshape(2, 64, width)
+    fields_in = keys_values.reshape(2, 2, 64, width)
+
+    first = pl.pallas_call(
+        prepare_first,
+        in_specs=[anywhere, anywhere, pl.BlockSpec(memory_space=pltpu.VMEM)],
+        out_specs=anywhere,
+        out_shape=jax.ShapeDtypeStruct((2, 2, height_count, 264, HEAD_DIM), bf16),
+        scratch_shapes=[
+            pltpu.VMEM((height_count, 2, 64, 3 * HEAD_DIM), bf16),
+            pltpu.VMEM((height_count, 2, 2, 64, 3 * HEAD_DIM), bf16),
+            pltpu.VMEM((2, 2, height_count, 264, HEAD_DIM), bf16),
+            pltpu.SemaphoreType.DMA((3, height_count)),
+        ],
+        compiler_params=params,
+        name="prepare_first",
+    )(queries_in, fields_in, far_cubes.reshape(2, heads, far_count).transpose(0, 2, 1))
+    second = pl.pallas_call(
+        prepare_second,
+        in_specs=[anywhere],
+        out_specs=anywhere,
+        out_shape=jax.ShapeDtypeStruct((2, 2, height_count, 32, HEAD_DIM), bf16),
+        scratch_shapes=[pltpu.SemaphoreType.DMA((2, height_count))],
+        compiler_params=params,
+        cost_estimate=pl.CostEstimate(flops=0, bytes_accessed=2**20, transcendentals=0),
+        name="prepare_second",
+    )(queries_in)
+
+    def exchange(x):
+        return lax.all_to_all(x, axes, 0, 0, tiled=True)
+
+    def swap(x, distance):
+        return lax.ppermute(x, "tm", [(i, i ^ distance) for i in range(tm_count)])
+
+    def attention(kernel, name, tokens, specs):
+        keys = devices * 128
+        work = devices * tokens * keys
+        return pl.pallas_call(
+            functools.partial(kernel, height_count),
+            in_specs=specs,
+            out_shape=jax.ShapeDtypeStruct((devices, tokens, HEAD_DIM), bf16),
+            scratch_shapes=[
+                pltpu.VMEM((2, devices, 2, 64, 2 * HEAD_DIM), bf16),
+                pltpu.VMEM((devices, tokens, HEAD_DIM), bf16),
+                pltpu.VMEM((devices, HEAD_DIM), f32),
+                pltpu.SemaphoreType.DMA((5, 4)),
+                pltpu.VMEM((ROWS, keys), f32),
+                pltpu.VMEM((ROWS, keys), f32),
+            ],
+            compiler_params=params,
+            cost_estimate=pl.CostEstimate(
+                flops=8 * work * HEAD_DIM, bytes_accessed=4 * 2**20, transcendentals=work
+            ),
+            name=name,
+        )
+
+    vmem = pl.BlockSpec(memory_space=pltpu.VMEM)
+    got_first = exchange(first.reshape(devices, 264, HEAD_DIM))
+    large = got_first[:, 64:192]
+    small = got_first[:, 192:256]
+    info = got_first[:, 256:264]
+    second, large = lax.optimization_barrier((second, large))
+    got_second = exchange(second.reshape(devices, 32, HEAD_DIM))
+    core_large = swap(large, 1)
+    chip = swap(small, 2)
+    core_small = swap(small, 1)
+    out_large = attention(large_kernel, "attend_large", 64, [anywhere, anywhere, vmem])(
+        got_first, core_large, info
+    )
+    core_chip = swap(chip, 1)
+
+    got_second, out_large = lax.optimization_barrier((got_second, out_large))
+    back_large = exchange(out_large)
+    out_small = attention(small_kernel, "attend_small", 32, [anywhere] * 5 + [vmem])(
+        got_first, got_second, chip, core_small, core_chip, info
+    )
+    back_large, out_small = lax.optimization_barrier((back_large, out_small))
+    back_small = exchange(out_small)
+    by_head = out_weight.reshape(height_count, 3, HEAD_DIM, width)
+    part, rest = pl.pallas_call(
+        project_large,
+        in_specs=[vmem, anywhere],
+        out_specs=(vmem, vmem),
+        out_shape=(
+            pltpu.VMEM((128, width), f32),
+            pltpu.VMEM((height_count, HEAD_DIM, width), bf16),
+        ),
+        scratch_shapes=[
+            pltpu.VMEM((2, height_count, HEAD_DIM, width), bf16),
+            pltpu.SemaphoreType.DMA((3, height_count)),
+        ],
+        compiler_params=pltpu.CompilerParams(vmem_limit_bytes=40 * 2**20),
+        cost_estimate=pl.CostEstimate(
+            flops=4 * 128 * width * width // 3, bytes_accessed=20 * 2**20, transcendentals=0
+        ),
+        name="project_large",
+    )(back_large, by_head)
+    back_small, part = lax.optimization_barrier((back_small, part))
+    output = pl.pallas_call(
+        project_small,
+        in_specs=[vmem, vmem, vmem],
+        out_shape=jax.ShapeDtypeStruct((128, width), bf16),
+        compiler_params=pltpu.CompilerParams(vmem_limit_bytes=40 * 2**20),
+        cost_estimate=pl.CostEstimate(
+            flops=2 * 128 * width * width // 3, bytes_accessed=8 * 2**20, transcendentals=0
+        ),
+        name="project_small",
+    )(back_small, rest, part)
+    return output.reshape(queries.shape)
+
+
 def solution(mesh):
     in_specs = (
         P("tm", "height", None, None, None),
@@ -142,4 +563,5 @@
         P(),
     )
     out_specs = P("tm", "height", None, None, None)
-    return jax.shard_map(body, mesh=mesh, in_specs=in_specs, out_specs=out_specs, check_vma=False)
+    fits = mesh.shape["tm"] == 4 and HEADS == 3 * mesh.shape["height"]
+    return jax.shard_map(by_heads if fits else body, mesh=mesh, in_specs=in_specs, out_specs=out_specs, check_vma=False)

time: 876 us -> 124 us (0.14)
  the two profiles are of different devices: /device:TPU:21 before, /device:TPU:0 now
where the time goes in v2:
time: 124 us; the launch traced here: 123 us
  waiting for transfers between devices  48.8 us (39%)
  Pallas kernels  45.6 us (37%)
  starting transfers between devices  20.6 us (17%)
  local copies, waits for them, and re-layouts  8.16 us (7%)
    all_to_all x4, waiting for transfers between devices, exchange(): return lax.all_to_all(x, axes, 0, 0, tiled=True)  46.7 us
    all_to_all x4, starting transfers between devices, exchange(): return lax.all_to_all(x, axes, 0, 0, tiled=True)  19.1 us
    pallas_call x1, Pallas kernels, by_heads(): attention(large_kernel, 'attend_large', 64, [anywhere, anywhere, vmem])  14.9 us
    pallas_call x1, Pallas kernels, by_heads(): attention(small_kernel, 'attend_small', 32, [anywhere] * 5 + [vmem])  9.65 us
    pallas_call x1, Pallas kernels, by_heads(): pl.pallas_call(prepare_second, in_specs=[anywhere], out_specs=anywhere, o...  9.19 us
    pallas_call x1, Pallas kernels, by_heads(): pl.pallas_call(project_large, in_specs=[vmem, anywhere], out_specs=(vmem,...  6.59 us
    unnamed x14, local copies, waits for them, and re-layouts  6.28 us
    pallas_call x1, Pallas kernels, by_heads(): pl.pallas_call(prepare_first, in_specs=[anywhere, anywhere, pl.BlockSpec(...  3.4 us
  transfers between devices with their start and end apart: 8, of which 5 were waited for; matrix products, arithmetic and copies ran while one was open for 1% of the time, Pallas kernels for 33%

profile of v2, /device:TPU:0, one launch (start us, length us, event | category | flops | bytes accessed | tf_op | source)
XLA Modules:
  0.0 123.3 jit_solution(6786990744712940646)
XLA Ops:
  0.0 3.4 %prepare_first.1 = bf16[2,2,8,264,128]{4,3,2,1,0:T(8,128)(2,1)} custom-call(bf16[2,64,3072]{2,1,0:T(8,128)(2,1)} %bitcast.11, bf16[2,2,64,3072]{3,2,1,0:T(8,128)(2,1)} %bitcast.13, s32[2,16,24]{2,1,0:T(8,128)} %bitcast.14), custom_call_target="tpu_custom_call" | custom-call | tf_op jit(solution)/shard_map/prepare_first/pallas_call | solution.py:450
  3.4 7.3 %all-to-all-start = ((bf16[32,264,128]{2,1,0:T(8,128)(2,1)}), bf16[32,264,128]{2,1,0:T(8,128)(2,1)S(1)}, u32[]{:S(2)}, u32[]{:S(2)}) async-start(bf16[32,264,128]{2,1,0:T(8,128)(2,1)} %bitcast.10), calls=%async_computation | async-start | bytes 4325376 | tf_op jit(solution)/shard_map/all_to_all | solution.py:476
  10.7 9.2 %prepare_second.1 = bf16[2,2,8,32,128]{4,3,2,1,0:T(8,128)(2,1)} custom-call(bf16[2,64,3072]{2,1,0:T(8,128)(2,1)} %bitcast.12), custom_call_target="tpu_custom_call" | custom-call | bytes 1048576 | tf_op jit(solution)/shard_map/prepare_second/pallas_call | solution.py:464
  19.9 42.3 %all-to-all-done.mine_ref.first_ref = bf16[32,264,128]{2,1,0:T(8,128)(2,1)S(1)} async-done(((bf16[32,264,128]{2,1,0:T(8,128)(2,1)}), bf16[32,264,128]{2,1,0:T(8,128)(2,1)S(1)}, u32[]{:S(2)}, u32[]{:S(2)}) %all-to-all-start) | async-done | bytes 2162720 | tf_op jit(solution)/shard_map/all_to_all | solution.py:476
  62.2 1.2 slice.12
  63.4 0.0 collective-permute-start
  63.4 0.1 slice.14
  63.5 0.9 collective-permute-start.1
  64.4 3.1 %all-to-all-start.1 = ((bf16[32,32,128]{2,1,0:T(8,128)(2,1)}), bf16[32,32,128]{2,1,0:T(8,128)(2,1)S(1)}, u32[]{:S(2)}, u32[]{:S(2)}) async-start(bf16[32,32,128]{2,1,0:T(8,128)(2,1)} %bitcast.5), calls=%async_computation.1 | async-start | bytes 524288 | tf_op jit(solution)/shard_map/all_to_all | solution.py:476
  67.5 0.6 slice.13.info_in
  68.1 0.0 collective-permute-done.core_ref
  68.1 0.0 copy-done.2
  68.1 14.9 %attend_large.1 = bf16[32,64,128]{2,1,0:T(8,128)(2,1)} custom-call(bf16[32,264,128]{2,1,0:T(8,128)(2,1)} %copy-done.2, bf16[32,128,128]{2,1,0:T(8,128)(2,1)} %collective-permute-done.core_ref, bf16[32,8,128]{2,1,0:T(8,128)(2,1)} %slice.13.info_in), custom_call_target="tpu_custom_call" | custom-call | flops 8589934592 | bytes 4194304 | tf_op jit(solution)/shard_map/attend_large/pallas_call | solution.py:513
  83.0 0.0 all-to-all-done.1.second_ref
  83.0 0.0 copy-start.3
  83.0 5.8 %all-to-all-start.2 = ((bf16[32,64,128]{2,1,0:T(8,128)(2,1)}), bf16[32,64,128]{2,1,0:T(8,128)(2,1)S(1)}, u32[]{:S(2)}, u32[]{:S(2)}) async-start(bf16[32,64,128]{2,1,0:T(8,128)(2,1)} %attend_large.1), calls=%async_computation.2 | async-start | bytes 1048576 | tf_op jit(solution)/shard_map/all_to_all | solution.py:476
  88.9 0.3 collective-permute-start.2
  89.2 0.0 collective-permute-done.1.chip_ref
  89.2 0.3 collective-permute-start.3
  89.5 1.4 %collective-permute-done.2.core_mine_ref = bf16[32,64,128]{2,1,0:T(8,128)(2,1)S(1)} collective-permute-done((bf16[32,64,128]{2,1,0:T(8,128)(2,1)S(1)}, bf16[32,64,128]{2,1,0:T(8,128)(2,1)S(1)}, u32[]{:S(2)}, u32[]{:S(2)}) %collective-permute-start.2) | collective-permute-done | bytes 524320 | tf_op jit(solution)/shard_map/ppermute | solution.py:479
  90.9 0.7 collective-permute-done.3.core_chip_ref
  91.6 0.0 copy-done.4
  91.6 0.0 copy-done.5
  91.6 0.8 copy-done.6
  92.4 9.7 %attend_small.1 = bf16[32,32,128]{2,1,0:T(8,128)(2,1)} custom-call(bf16[32,264,128]{2,1,0:T(8,128)(2,1)} %copy-done.2, bf16[32,32,128]{2,1,0:T(8,128)(2,1)} %copy-done.3, bf16[32,64,128]{2,1,0:T(8,128)(2,1)} %copy-done.4, bf16[32,64,128]{2,1,0:T(8,128)(2,1)} %copy-done.5, bf16[32,64,128]{2,1,0:T(8,128)(2,1)} %copy-done.6, bf16[32,8,128]{2,1,0:T(8,128)(2,1)} %slice.13.info_in), custom_call_target="tpu_custom_call" | custom-call | flops 4294967296 | bytes 4194304 | tf_op jit(solution)/shard_map/attend_small/pallas_call | solution.py:520
  102.1 3.1 %all-to-all-done.2.back_ref = bf16[32,64,128]{2,1,0:T(8,128)(2,1)S(1)} async-done(((bf16[32,64,128]{2,1,0:T(8,128)(2,1)}), bf16[32,64,128]{2,1,0:T(8,128)(2,1)S(1)}, u32[]{:S(2)}, u32[]{:S(2)}) %all-to-all-start.2) | async-done | bytes 524320 | tf_op jit(solution)/shard_map/all_to_all | solution.py:476
  105.2 2.9 %all-to-all-start.3 = ((bf16[32,32,128]{2,1,0:T(8,128)(2,1)}), bf16[32,32,128]{2,1,0:T(8,128)(2,1)S(1)}, u32[]{:S(2)}, u32[]{:S(2)}) async-start(bf16[32,32,128]{2,1,0:T(8,128)(2,1)} %attend_small.1), calls=%async_computation.3 | async-start | bytes 524288 | tf_op jit(solution)/shard_map/all_to_all | solution.py:476
  108.1 6.6 %project_large.1 = (f32[128,3072]{1,0:T(8,128)S(1)}, bf16[8,128,3072]{2,1,0:T(8,128)(2,1)S(1)}) custom-call(bf16[32,64,128]{2,1,0:T(8,128)(2,1)S(1)} %all-to-all-done.2.back_ref, bf16[8,3,128,3072]{3,2,1,0:T(8,128)(2,1)} %bitcast.9), custom_call_target="tpu_custom_call" | custom-call | flops 1610612736 | bytes 20971520 | tf_op jit(solution)/shard_map/project_large/pallas_call | solution.py:526
  114.7 2.7 %copy-done = bf16[8,128,3072]{2,1,0:T(8,128)(2,1)} copy-done((bf16[8,128,3072]{2,1,0:T(8,128)(2,1)}, bf16[8,128,3072]{2,1,0:T(8,128)(2,1)S(1)}, u32[]{:S(2)}) %copy-start) | copy-done | bytes 6291480
  117.4 1.2 all-to-all-done.3.back_ref
  118.6 2.8 %copy-done.1 = bf16[8,128,3072]{2,1,0:T(8,128)(2,1)S(1)} copy-done((bf16[8,128,3072]{2,1,0:T(8,128)(2,1)S(1)}, bf16[8,128,3072]{2,1,0:T(8,128)(2,1)}, u32[]{:S(2)}) %copy-start.1) | copy-done | bytes 6291480
  121.4 1.9 %project_small.1 = bf16[128,3072]{1,0:T(8,128)(2,1)} custom-call(bf16[32,32,128]{2,1,0:T(8,128)(2,1)S(1)} %all-to-all-done.3.back_ref, bf16[8,128,3072]{2,1,0:T(8,128)(2,1)S(1)} %copy-done.1, f32[128,3072]{1,0:T(8,128)S(1)} %get-tuple-element.24.part_ref), custom_call_target="tpu_custom_call" | custom-call | flops 805306368 | bytes 8388608 | tf_op jit(solution)/shard_map/project_small/pallas_call | solution.py:545
  (7 shorter events, 0.0 us)
Async XLA Ops:
  3.4 58.8 %all-to-all-start = ((bf16[32,264,128]{2,1,0:T(8,128)(2,1)}), bf16[32,264,128]{2,1,0:T(8,128)(2,1)S(1)}, u32[]{:S(2)}, u32[]{:S(2)}) async-start(bf16[32,264,128]{2,1,0:T(8,128)(2,1)} %bitcast.10), calls=%async_computation | async-start | bytes 4325376 | tf_op jit(solution)/shard_map/all_to_all | solution.py:476
  62.2 5.9 %copy-start.2 = (bf16[32,264,128]{2,1,0:T(8,128)(2,1)}, bf16[32,264,128]{2,1,0:T(8,128)(2,1)S(1)}, u32[]{:S(2)}) copy-start(bf16[32,264,128]{2,1,0:T(8,128)(2,1)S(1)} %all-to-all-done.mine_ref.first_ref) | copy-start | bytes 6488068
  63.4 4.7 %collective-permute-start = (bf16[32,128,128]{2,1,0:T(8,128)(2,1)}, bf16[32,128,128]{2,1,0:T(8,128)(2,1)}, u32[]{:S(2)}, u32[]{:S(2)}) collective-permute-start(bf16[32,128,128]{2,1,0:T(8,128)(2,1)} %slice.12), channel_id=1, source_target_pairs={{0,8},{8,0},{16,24},{24,16},{1,9},{9,1},{17,25},{25,17},{2,10},{10... | collective-permute-start | bytes 3145736 | tf_op jit(solution)/shard_map/ppermute | solution.py:479
  63.5 25.7 %collective-permute-start.1 = (bf16[32,64,128]{2,1,0:T(8,128)(2,1)S(1)}, bf16[32,64,128]{2,1,0:T(8,128)(2,1)S(1)}, u32[]{:S(2)}, u32[]{:S(2)}) collective-permute-start(bf16[32,64,128]{2,1,0:T(8,128)(2,1)S(1)} %slice.14), channel_id=1, source_target_pairs={{0,16},{8,24},{16,0},{24,8},{1,17},{9,25},{17,1},{25,9},{2,18},{10... | collective-permute-start | bytes 1572872 | tf_op jit(solution)/shard_map/ppermute | solution.py:479
  64.4 18.6 %all-to-all-start.1 = ((bf16[32,32,128]{2,1,0:T(8,128)(2,1)}), bf16[32,32,128]{2,1,0:T(8,128)(2,1)S(1)}, u32[]{:S(2)}, u32[]{:S(2)}) async-start(bf16[32,32,128]{2,1,0:T(8,128)(2,1)} %bitcast.5), calls=%async_computation.1 | async-start | bytes 524288 | tf_op jit(solution)/shard_map/all_to_all | solution.py:476
  83.0 8.6 %copy-start.3 = (bf16[32,32,128]{2,1,0:T(8,128)(2,1)}, bf16[32,32,128]{2,1,0:T(8,128)(2,1)S(1)}, u32[]{:S(2)}) copy-start(bf16[32,32,128]{2,1,0:T(8,128)(2,1)S(1)} %all-to-all-done.1.second_ref) | copy-start | bytes 786436
  83.0 22.2 %all-to-all-start.2 = ((bf16[32,64,128]{2,1,0:T(8,128)(2,1)}), bf16[32,64,128]{2,1,0:T(8,128)(2,1)S(1)}, u32[]{:S(2)}, u32[]{:S(2)}) async-start(bf16[32,64,128]{2,1,0:T(8,128)(2,1)} %attend_large.1), calls=%async_computation.2 | async-start | bytes 1048576 | tf_op jit(solution)/shard_map/all_to_all | solution.py:476
  88.9 2.0 %collective-permute-start.2 = (bf16[32,64,128]{2,1,0:T(8,128)(2,1)S(1)}, bf16[32,64,128]{2,1,0:T(8,128)(2,1)S(1)}, u32[]{:S(2)}, u32[]{:S(2)}) collective-permute-start(bf16[32,64,128]{2,1,0:T(8,128)(2,1)S(1)} %slice.14), channel_id=1, source_target_pairs={{0,8},{8,0},{16,24},{24,16},{1,9},{9,1},{17,25},{25,17},{2,10},{10... | collective-permute-start | bytes 1572872 | tf_op jit(solution)/shard_map/ppermute | solution.py:479
  89.2 2.4 %copy-start.4 = (bf16[32,64,128]{2,1,0:T(8,128)(2,1)}, bf16[32,64,128]{2,1,0:T(8,128)(2,1)S(1)}, u32[]{:S(2)}) copy-start(bf16[32,64,128]{2,1,0:T(8,128)(2,1)S(1)} %collective-permute-done.1.chip_ref) | copy-start | bytes 1572868
  89.2 2.4 %collective-permute-start.3 = (bf16[32,64,128]{2,1,0:T(8,128)(2,1)S(1)}, bf16[32,64,128]{2,1,0:T(8,128)(2,1)S(1)}, u32[]{:S(2)}, u32[]{:S(2)}) collective-permute-start(bf16[32,64,128]{2,1,0:T(8,128)(2,1)S(1)} %collective-permute-done.1.chip_ref), channel_id=1, source_target_pairs={{0,8},{8,0},{16,24},{24,16},{1,9},{9,1},{17,25},{25,17},{2,10},{10... | collective-permute-start | bytes 1572872 | tf_op jit(solution)/shard_map/ppermute | solution.py:479
  90.9 0.8 copy-start.5
  91.6 0.8 copy-start.6
  105.2 13.4 %all-to-all-start.3 = ((bf16[32,32,128]{2,1,0:T(8,128)(2,1)}), bf16[32,32,128]{2,1,0:T(8,128)(2,1)S(1)}, u32[]{:S(2)}, u32[]{:S(2)}) async-start(bf16[32,32,128]{2,1,0:T(8,128)(2,1)} %attend_small.1), calls=%async_computation.3 | async-start | bytes 524288 | tf_op jit(solution)/shard_map/all_to_all | solution.py:476
  114.7 2.7 %copy-start = (bf16[8,128,3072]{2,1,0:T(8,128)(2,1)}, bf16[8,128,3072]{2,1,0:T(8,128)(2,1)S(1)}, u32[]{:S(2)}) copy-start(bf16[8,128,3072]{2,1,0:T(8,128)(2,1)S(1)} %get-tuple-element.23.weight_ref) | copy-start | bytes 18874372
  118.6 2.8 %copy-start.1 = (bf16[8,128,3072]{2,1,0:T(8,128)(2,1)S(1)}, bf16[8,128,3072]{2,1,0:T(8,128)(2,1)}, u32[]{:S(2)}) copy-start(bf16[8,128,3072]{2,1,0:T(8,128)(2,1)} %copy-done) | copy-start | bytes 18874372

commit v3 on v2

--- a/solution.py
+++ b/solution.py
@@ -283,14 +283,17 @@
         first = index * 2 * step
         later = score(first + step, scores[1])
         mix(first, scores[0], largest)
-        following = jnp.minimum(first + 2 * step, sources - step)
-        largest = score(following, scores[0])
+        largest = score(first + 2 * step, scores[0])
         mix(first + step, scores[1], later)
         return largest
 
     largest = score(0, scores[0])
     wait_values()
-    lax.fori_loop(0, sources // step // 2, two_blocks, largest)
+    largest = lax.fori_loop(0, sources // step // 2 - 1, two_blocks, largest)
+    last = sources - step
+    later = score(last, scores[1])
+    mix(last - step, scores[0], largest)
+    mix(last, scores[1], later)
 
 
 def pieces(count, source, target, sems, row):
@@ -321,7 +324,7 @@
     other = [
         pieces(
             count,
-            lambda at, k=k: core_ref.at[at, 64 * k : 64 + 64 * k, :],
+            lambda at, k=k: core_ref.at[at, 64 + 64 * k : 128 + 64 * k, :],
             lambda at, k=k: kv_ref.at[k, at, 1 - core, :, 0:HEAD_DIM],
             sems,
             2 + k,
@@ -347,7 +350,7 @@
 
 
 def small_kernel(
-    height_count, first_ref, second_ref, chip_ref, core_mine_ref, core_chip_ref, info_in, out_ref,
+    height_count, first_ref, second_ref, chip_ref, core_first_ref, core_chip_ref, info_in, out_ref,
     kv_ref, q_in, bias_ref, sems, *scores
 ):
     core = lax.axis_index("tm") % 2
@@ -362,7 +365,7 @@
     copies = pieces(count, lambda at: second_ref.at[at], lambda at: q_in.at[at], sems, 4)
     copies += kept(lambda at: first_ref.at[at, 192:256, :], chip, core, 0)
     copies += kept(lambda at: chip_ref.at[at], 1 - chip, core, 1)
-    copies += kept(lambda at: core_mine_ref.at[at], chip, 1 - core, 2)
+    copies += kept(lambda at: core_first_ref.at[at, 192:256, :], chip, 1 - core, 2)
     copies += kept(lambda at: core_chip_ref.at[at], 1 - chip, 1 - core, 3)
     for copy in copies:
         copy.start()
@@ -377,7 +380,11 @@
     attend(q_at, lambda: None, kv_ref, bias_ref, out_ref, scores)
 
 
-def project_large(back_ref, weight_ref, part_ref, rest_ref, weights, sems):
+def side_by_side(refs, rows):
+    return jnp.concatenate([jnp.concatenate([refs[i] for i in row], axis=1) for row in rows], axis=0)
+
+
+def project_large(back_ref, weight_ref, part_ref, weights, sems):
     groups = back_ref.shape[0] // 4
 
     def copies(g):
@@ -386,51 +393,53 @@
             for chip in range(2)
         ]
 
-    def rest(g):
-        return pltpu.make_async_copy(weight_ref.at[g, 1], rest_ref.at[g], sems.at[2, g])
-
     for g in range(groups):
         for copy in copies(g):
             copy.start()
-    for g in range(groups):
-        rest(g).start()
     total = None
     for g in range(0, groups, 2):
         for copy in copies(g) + copies(g + 1):
             copy.wait()
         for chip in range(2):
-            rows = [
-                jnp.concatenate(
-                    [back_ref[(chip * 2 + core) * groups + g + i] for i in range(2)], axis=1
-                )
-                for core in range(2)
-            ]
+            first = chip * 2 * groups + g
+            rows = [[first + core * groups + i for i in range(2)] for core in range(2)]
             part = jnp.dot(
-                jnp.concatenate(rows, axis=0),
+                side_by_side(back_ref, rows),
                 weights[chip, g : g + 2].reshape(2 * HEAD_DIM, weights.shape[-1]),
                 preferred_element_type=jnp.float32,
             )
             total = part if total is None else total + part
     part_ref[...] = total
-    for g in range(groups):
-        rest(g).wait()
-
-
-def project_small(back_ref, weight_ref, part_ref, out_ref):
+
+
+def project_small(back_ref, weight_ref, part_ref, out_ref, weights, sems):
     groups = back_ref.shape[0] // 4
-    rows = [
-        jnp.concatenate([back_ref[to * groups + g] for g in range(groups)], axis=1)
-        for to in (0, 2, 1, 3)
-    ]
-    attended = jnp.concatenate(rows, axis=0)
-    width = out_ref.shape[-1]
-    tile = width // 4
-    for start in range(0, width, tile):
-        weight = weight_ref[:, :, start : start + tile].reshape(groups * HEAD_DIM, tile)
-        total = part_ref[:, start : start + tile] + jnp.dot(
-            attended, weight, preferred_element_type=jnp.float32
-        )
-        out_ref[:, start : start + tile] = total.astype(out_ref.dtype)
+    tiles = sems.shape[0]
+    tile = weights.shape[-1]
+
+    def copies(n):
+        return [
+            pltpu.make_async_copy(
+                weight_ref.at[g, 1, :, n * tile : (n + 1) * tile], weights.at[n, g], sems.at[n, g]
+            )
+            for g in range(groups)
+        ]
+
+    for n in range(tiles):
+        for copy in copies(n):
+            copy.start()
+    rows = [[to * groups + g for g in range(groups)] for to in (0, 2, 1, 3)]
+    attended = side_by_side(back_ref, rows)
+    for n in range(tiles):
+        for copy in copies(n):
+            copy.wait()
+        lanes = slice(n * tile, (n + 1) * tile)
+        total = part_ref[:, lanes] + jnp.dot(
+            attended,
+            weights[n].reshape(groups * HEAD_DIM, tile),
+            preferred_element_type=jnp.float32,
+        )
+        out_ref[:, lanes] = total.astype(out_ref.dtype)
 
 
 def by_heads(queries, keys_values, far_cubes, out_weight):
@@ -442,8 +451,9 @@
     far_count = far_cubes.shape[-1]
     axes = ("tm", "height")
     bf16, f32 = jnp.bfloat16, jnp.float32
-    params = pltpu.CompilerParams(vmem_limit_bytes=60 * 2**20)
-    anywhere = pl.BlockSpec(memory_space=pl.ANY)
+    params = pltpu.CompilerParams(vmem_limit_bytes=24 * 2**20)
+    alone = pltpu.CompilerParams(vmem_limit_bytes=60 * 2**20)
+    anywhere = pl.BlockSpec(memory_space=pltpu.HBM)
     queries_in = queries.reshape(2, 64, width)
     fields_in = keys_values.reshape(2, 2, 64, width)
 
@@ -458,7 +468,7 @@
             pltpu.VMEM((2, 2, height_count, 264, HEAD_DIM), bf16),
             pltpu.SemaphoreType.DMA((3, height_count)),
         ],
-        compiler_params=params,
+        compiler_params=alone,
         name="prepare_first",
     )(queries_in, fields_in, far_cubes.reshape(2, heads, far_count).transpose(0, 2, 1))
     second = pl.pallas_call(
@@ -467,7 +477,7 @@
         out_specs=anywhere,
         out_shape=jax.ShapeDtypeStruct((2, 2, height_count, 32, HEAD_DIM), bf16),
         scratch_shapes=[pltpu.SemaphoreType.DMA((2, height_count))],
-        compiler_params=params,
+        compiler_params=alone,
         cost_estimate=pl.CostEstimate(flops=0, bytes_accessed=2**20, transcendentals=0),
         name="prepare_second",
     )(queries_in)
@@ -502,56 +512,55 @@
 
     vmem = pl.BlockSpec(memory_space=pltpu.VMEM)
     got_first = exchange(first.reshape(devices, 264, HEAD_DIM))
-    large = got_first[:, 64:192]
+    got_first, second = lax.optimization_barrier((got_first, second))
     small = got_first[:, 192:256]
     info = got_first[:, 256:264]
-    second, large = lax.optimization_barrier((second, large))
+    second, small = lax.optimization_barrier((second, small))
     got_second = exchange(second.reshape(devices, 32, HEAD_DIM))
-    core_large = swap(large, 1)
+    core_first = swap(got_first, 1)
     chip = swap(small, 2)
-    core_small = swap(small, 1)
     out_large = attention(large_kernel, "attend_large", 64, [anywhere, anywhere, vmem])(
-        got_first, core_large, info
+        got_first, core_first, info
     )
     core_chip = swap(chip, 1)
 
     got_second, out_large = lax.optimization_barrier((got_second, out_large))
     back_large = exchange(out_large)
     out_small = attention(small_kernel, "attend_small", 32, [anywhere] * 5 + [vmem])(
-        got_first, got_second, chip, core_small, core_chip, info
+        got_first, got_second, chip, core_first, core_chip, info
     )
     back_large, out_small = lax.optimization_barrier((back_large, out_small))
     back_small = exchange(out_small)
     by_head = out_weight.reshape(height_count, 3, HEAD_DIM, width)
-    part, rest = pl.pallas_call(
+    part = pl.pallas_call(
         project_large,
         in_specs=[vmem, anywhere],
-        out_specs=(vmem, vmem),
-        out_shape=(
-            pltpu.VMEM((128, width), f32),
-            pltpu.VMEM((height_count, HEAD_DIM, width), bf16),
-        ),
+        out_shape=pltpu.VMEM((128, width), f32),
         scratch_shapes=[
             pltpu.VMEM((2, height_count, HEAD_DIM, width), bf16),
-            pltpu.SemaphoreType.DMA((3, height_count)),
+            pltpu.SemaphoreType.DMA((2, height_count)),
         ],
-        compiler_params=pltpu.CompilerParams(vmem_limit_bytes=40 * 2**20),
+        compiler_params=pltpu.CompilerParams(vmem_limit_bytes=50 * 2**20),
         cost_estimate=pl.CostEstimate(
-            flops=4 * 128 * width * width // 3, bytes_accessed=20 * 2**20, transcendentals=0
+            flops=4 * 128 * width * width // 3, bytes_accessed=14 * 2**20, transcendentals=0
         ),
         name="project_large",
     )(back_large, by_head)
     back_small, part = lax.optimization_barrier((back_small, part))
     output = pl.pallas_call(
         project_small,
-        in_specs=[vmem, vmem, vmem],
+        in_specs=[vmem, anywhere, vmem],
         out_shape=jax.ShapeDtypeStruct((128, width), bf16),
-        compiler_params=pltpu.CompilerParams(vmem_limit_bytes=40 * 2**20),
+        scratch_shapes=[
+            pltpu.VMEM((6, height_count, HEAD_DIM, width // 6), bf16),
+            pltpu.SemaphoreType.DMA((6, height_count)),
+        ],
+        compiler_params=pltpu.CompilerParams(vmem_limit_bytes=50 * 2**20),
         cost_estimate=pl.CostEstimate(
             flops=2 * 128 * width * width // 3, bytes_accessed=8 * 2**20, transcendentals=0
         ),
         name="project_small",
-    )(back_small, rest, part)
+    )(back_small, by_head, part)
     return output.reshape(queries.shape)
 
 

time: 124 us -> 120 us (0.968)
  waiting for transfers between devices: 48.8 us -> 56.1 us
  local copies, waits for them, and re-layouts: 8.16 us -> 0.86 us
  Pallas kernels: 45.6 us -> 42.5 us
    all_to_all x4, waiting for transfers between devices: 46.7 us -> 54.3 us  [exchange(): return lax.all_to_all(x, axes, 0, 0, tiled=True)]
    unnamed x14 -> x0, local copies, waits for them, and re-layouts: 6.28 us -> none
    pallas_call x1, Pallas kernels: 14.9 us -> 12.6 us  [by_heads(): attention(large_kernel, 'attend_large', 64, [anywhere, anywhere, vmem])]
    pallas_call x1, Pallas kernels: 9.65 us -> 7.54 us  [by_heads(): attention(small_kernel, 'attend_small', 32, [anywhere] * 5 + [vmem])]
    pallas_call x2, Pallas kernels: 8.47 us -> 9.84 us  [the longest x1 5.32 us: by_heads(): pl.pallas_call(project_large, in_specs=[vmem, anywhere], out_shape=pltpu....]
  transfers between devices with their start and end apart: 8 -> 7, of which waited for: 5 -> 4; matrix products, arithmetic and copies ran while one was open for 1% -> 1% of each run, Pallas kernels for 33% -> 29%
where the time goes in v3:
time: 120 us
  waiting for transfers between devices  56.1 us (47%)
  Pallas kernels  42.5 us (35%)
  starting transfers between devices  20.1 us (17%)
    all_to_all x4, waiting for transfers between devices, exchange(): return lax.all_to_all(x, axes, 0, 0, tiled=True)  54.3 us
    all_to_all x4, starting transfers between devices, exchange(): return lax.all_to_all(x, axes, 0, 0, tiled=True)  18.1 us
    pallas_call x1, Pallas kernels, by_heads(): attention(large_kernel, 'attend_large', 64, [anywhere, anywhere, vmem])  12.6 us
    pallas_call x1, Pallas kernels, by_heads(): pl.pallas_call(prepare_second, in_specs=[anywhere], out_specs=anywhere, o...  9.19 us
    pallas_call x1, Pallas kernels, by_heads(): attention(small_kernel, 'attend_small', 32, [anywhere] * 5 + [vmem])  7.54 us
    pallas_call x1, Pallas kernels, by_heads(): pl.pallas_call(project_large, in_specs=[vmem, anywhere], out_shape=pltpu....  5.32 us
    pallas_call x1, Pallas kernels, by_heads(): pl.pallas_call(project_small, in_specs=[vmem, anywhere, vmem], out_shape=...  4.52 us
    pallas_call x1, Pallas kernels, by_heads(): pl.pallas_call(prepare_first, in_specs=[anywhere, anywhere, pl.BlockSpec(...  3.41 us
  transfers between devices with their start and end apart: 7, of which 4 were waited for; matrix products, arithmetic and copies ran while one was open for 1% of the time, Pallas kernels for 29%

profile of v3, /device:TPU:0, one launch (start us, length us, event | category | flops | bytes accessed | tf_op | source)
XLA Modules:
  0.0 119.9 jit_solution(430737659721658006)
XLA Ops:
  0.0 3.4 %prepare_first.1 = bf16[2,2,8,264,128]{4,3,2,1,0:T(8,128)(2,1)} custom-call(bf16[2,64,3072]{2,1,0:T(8,128)(2,1)} %bitcast.12, bf16[2,2,64,3072]{3,2,1,0:T(8,128)(2,1)} %bitcast.14, s32[2,16,24]{2,1,0:T(8,128)} %bitcast.16), custom_call_target="tpu_custom_call" | custom-call | tf_op jit(solution)/shard_map/prepare_first/pallas_call | solution.py:460
  3.4 7.3 %all-to-all-start = ((bf16[32,264,128]{2,1,0:T(8,128)(2,1)}), bf16[32,264,128]{2,1,0:T(8,128)(2,1)S(1)}, u32[]{:S(2)}, u32[]{:S(2)}) async-start(bf16[32,264,128]{2,1,0:T(8,128)(2,1)} %bitcast.11), calls=%async_computation | async-start | bytes 4325376 | tf_op jit(solution)/shard_map/all_to_all | solution.py:486
  10.7 9.2 %prepare_second.1 = bf16[2,2,8,32,128]{4,3,2,1,0:T(8,128)(2,1)} custom-call(bf16[2,64,3072]{2,1,0:T(8,128)(2,1)} %bitcast.13), custom_call_target="tpu_custom_call" | custom-call | bytes 1048576 | tf_op jit(solution)/shard_map/prepare_second/pallas_call | solution.py:474
  19.9 42.3 %all-to-all-done.mine_ref.first_ref = bf16[32,264,128]{2,1,0:T(8,128)(2,1)S(1)} async-done(((bf16[32,264,128]{2,1,0:T(8,128)(2,1)}), bf16[32,264,128]{2,1,0:T(8,128)(2,1)S(1)}, u32[]{:S(2)}, u32[]{:S(2)}) %all-to-all-start) | async-done | bytes 2162720 | tf_op jit(solution)/shard_map/all_to_all | solution.py:486
  62.2 0.0 collective-permute-start
  62.2 0.9 slice.6
  63.1 3.4 %all-to-all-start.1 = ((bf16[32,32,128]{2,1,0:T(8,128)(2,1)}), bf16[32,32,128]{2,1,0:T(8,128)(2,1)S(1)}, u32[]{:S(2)}, u32[]{:S(2)}) async-start(bf16[32,32,128]{2,1,0:T(8,128)(2,1)} %bitcast.15), calls=%async_computation.1 | async-start | bytes 524288 | tf_op jit(solution)/shard_map/all_to_all | solution.py:486
  66.5 1.8 %collective-permute-start.1 = (bf16[32,64,128]{2,1,0:T(8,128)(2,1)}, bf16[32,64,128]{2,1,0:T(8,128)(2,1)S(1)}, u32[]{:S(2)}, u32[]{:S(2)}) collective-permute-start(bf16[32,64,128]{2,1,0:T(8,128)(2,1)} %slice.6), channel_id=1, source_target_pairs={{0,16},{8,24},{16,0},{24,8},{1,17},{9,25},{17,1},{25,9},{2,18},{10... | collective-permute-start | bytes 1572872 | tf_op jit(solution)/shard_map/ppermute | solution.py:489
  68.3 0.0 collective-permute-done.core_ref.core_first_ref
  68.3 12.6 %attend_large.1 = bf16[32,64,128]{2,1,0:T(8,128)(2,1)} custom-call(bf16[32,264,128]{2,1,0:T(8,128)(2,1)S(1)} %all-to-all-done.mine_ref.first_ref, bf16[32,264,128]{2,1,0:T(8,128)(2,1)} %collective-permute-done.core_ref.core_first_ref, bf16[32,8,128]{2,1,0:T(8,128)(2,1)S(1)} %slice.7.info_in), custom_call_target="tpu_custom_call" | custom-call | flops 8589934592 | bytes 4194304 | tf_op jit(solution)/shard_map/attend_large/pallas_call | solution.py:522
  80.9 0.0 all-to-all-done.1.second_ref
  80.9 4.8 %all-to-all-start.2 = ((bf16[32,64,128]{2,1,0:T(8,128)(2,1)}), bf16[32,64,128]{2,1,0:T(8,128)(2,1)S(1)}, u32[]{:S(2)}, u32[]{:S(2)}) async-start(bf16[32,64,128]{2,1,0:T(8,128)(2,1)} %attend_large.1), calls=%async_computation.2 | async-start | bytes 1048576 | tf_op jit(solution)/shard_map/all_to_all | solution.py:486
  85.8 0.0 collective-permute-done.1.chip_ref
  85.8 0.1 collective-permute-start.2
  85.9 1.8 %collective-permute-done.2.core_chip_ref = bf16[32,64,128]{2,1,0:T(8,128)(2,1)S(1)} collective-permute-done((bf16[32,64,128]{2,1,0:T(8,128)(2,1)S(1)}, bf16[32,64,128]{2,1,0:T(8,128)(2,1)S(1)}, u32[]{:S(2)}, u32[]{:S(2)}) %collective-permute-start.2) | collective-permute-done | bytes 524320 | tf_op jit(solution)/shard_map/ppermute | solution.py:489
  87.7 7.5 %attend_small.1 = bf16[32,32,128]{2,1,0:T(8,128)(2,1)} custom-call(bf16[32,264,128]{2,1,0:T(8,128)(2,1)S(1)} %all-to-all-done.mine_ref.first_ref, bf16[32,32,128]{2,1,0:T(8,128)(2,1)S(1)} %all-to-all-done.1.second_ref, bf16[32,64,128]{2,1,0:T(8,128)(2,1)S(1)} %collective-permute-done.1.chip_ref, ...), custom_call_target="tpu_custom_call" | custom-call | flops 4294967296 | bytes 4194304 | tf_op jit(solution)/shard_map/attend_small/pallas_call | solution.py:529
  95.3 6.6 %all-to-all-done.2.back_ref = bf16[32,64,128]{2,1,0:T(8,128)(2,1)S(1)} async-done(((bf16[32,64,128]{2,1,0:T(8,128)(2,1)}), bf16[32,64,128]{2,1,0:T(8,128)(2,1)S(1)}, u32[]{:S(2)}, u32[]{:S(2)}) %all-to-all-start.2) | async-done | bytes 524320 | tf_op jit(solution)/shard_map/all_to_all | solution.py:486
  101.9 2.6 %all-to-all-start.3 = ((bf16[32,32,128]{2,1,0:T(8,128)(2,1)}), bf16[32,32,128]{2,1,0:T(8,128)(2,1)S(1)}, u32[]{:S(2)}, u32[]{:S(2)}) async-start(bf16[32,32,128]{2,1,0:T(8,128)(2,1)} %attend_small.1), calls=%async_computation.3 | async-start | bytes 524288 | tf_op jit(solution)/shard_map/all_to_all | solution.py:486
  104.5 5.3 %project_large.1.part_ref = f32[128,3072]{1,0:T(8,128)S(1)} custom-call(bf16[32,64,128]{2,1,0:T(8,128)(2,1)S(1)} %all-to-all-done.2.back_ref, bf16[8,3,128,3072]{3,2,1,0:T(8,128)(2,1)} %bitcast.9), custom_call_target="tpu_custom_call" | custom-call | flops 1610612736 | bytes 14680064 | tf_op jit(solution)/shard_map/project_large/pallas_call | solution.py:535
  109.8 5.3 %all-to-all-done.3.back_ref = bf16[32,32,128]{2,1,0:T(8,128)(2,1)S(1)} async-done(((bf16[32,32,128]{2,1,0:T(8,128)(2,1)}), bf16[32,32,128]{2,1,0:T(8,128)(2,1)S(1)}, u32[]{:S(2)}, u32[]{:S(2)}) %all-to-all-start.3) | async-done | bytes 262176 | tf_op jit(solution)/shard_map/all_to_all | solution.py:486
  115.2 4.5 %project_small.1 = bf16[128,3072]{1,0:T(8,128)(2,1)} custom-call(bf16[32,32,128]{2,1,0:T(8,128)(2,1)S(1)} %all-to-all-done.3.back_ref, bf16[8,3,128,3072]{3,2,1,0:T(8,128)(2,1)} %bitcast.10, f32[128,3072]{1,0:T(8,128)S(1)} %project_large.1.part_ref), custom_call_target="tpu_custom_call" | custom-call | flops 805306368 | bytes 8388608 | tf_op jit(solution)/shard_map/project_small/pallas_call | solution.py:550
  (1 shorter events, 0.0 us)
Async XLA Ops:
  3.4 58.8 %all-to-all-start = ((bf16[32,264,128]{2,1,0:T(8,128)(2,1)}), bf16[32,264,128]{2,1,0:T(8,128)(2,1)S(1)}, u32[]{:S(2)}, u32[]{:S(2)}) async-start(bf16[32,264,128]{2,1,0:T(8,128)(2,1)} %bitcast.11), calls=%async_computation | async-start | bytes 4325376 | tf_op jit(solution)/shard_map/all_to_all | solution.py:486
  62.2 6.1 %collective-permute-start = (bf16[32,264,128]{2,1,0:T(8,128)(2,1)S(1)}, bf16[32,264,128]{2,1,0:T(8,128)(2,1)}, u32[]{:S(2)}, u32[]{:S(2)}) collective-permute-start(bf16[32,264,128]{2,1,0:T(8,128)(2,1)S(1)} %all-to-all-done.mine_ref.first_ref), channel_id=1, source_target_pairs={{0,8},{8,0},{16,24},{24,16},{1,9},{9,1},{17,25},{25,17},{2,10},{10... | collective-permute-start | bytes 6488072 | tf_op jit(solution)/shard_map/ppermute | solution.py:489
  63.1 17.8 %all-to-all-start.1 = ((bf16[32,32,128]{2,1,0:T(8,128)(2,1)}), bf16[32,32,128]{2,1,0:T(8,128)(2,1)S(1)}, u32[]{:S(2)}, u32[]{:S(2)}) async-start(bf16[32,32,128]{2,1,0:T(8,128)(2,1)} %bitcast.15), calls=%async_computation.1 | async-start | bytes 524288 | tf_op jit(solution)/shard_map/all_to_all | solution.py:486
  66.5 19.2 %collective-permute-start.1 = (bf16[32,64,128]{2,1,0:T(8,128)(2,1)}, bf16[32,64,128]{2,1,0:T(8,128)(2,1)S(1)}, u32[]{:S(2)}, u32[]{:S(2)}) collective-permute-start(bf16[32,64,128]{2,1,0:T(8,128)(2,1)} %slice.6), channel_id=1, source_target_pairs={{0,16},{8,24},{16,0},{24,8},{1,17},{9,25},{17,1},{25,9},{2,18},{10... | collective-permute-start | bytes 1572872 | tf_op jit(solution)/shard_map/ppermute | solution.py:489
  80.9 21.0 %all-to-all-start.2 = ((bf16[32,64,128]{2,1,0:T(8,128)(2,1)}), bf16[32,64,128]{2,1,0:T(8,128)(2,1)S(1)}, u32[]{:S(2)}, u32[]{:S(2)}) async-start(bf16[32,64,128]{2,1,0:T(8,128)(2,1)} %attend_large.1), calls=%async_computation.2 | async-start | bytes 1048576 | tf_op jit(solution)/shard_map/all_to_all | solution.py:486
  85.8 2.0 %collective-permute-start.2 = (bf16[32,64,128]{2,1,0:T(8,128)(2,1)S(1)}, bf16[32,64,128]{2,1,0:T(8,128)(2,1)S(1)}, u32[]{:S(2)}, u32[]{:S(2)}) collective-permute-start(bf16[32,64,128]{2,1,0:T(8,128)(2,1)S(1)} %collective-permute-done.1.chip_ref), channel_id=1, source_target_pairs={{0,8},{8,0},{16,24},{24,16},{1,9},{9,1},{17,25},{25,17},{2,10},{10... | collective-permute-start | bytes 1572872 | tf_op jit(solution)/shard_map/ppermute | solution.py:489
  101.9 13.2 %all-to-all-start.3 = ((bf16[32,32,128]{2,1,0:T(8,128)(2,1)}), bf16[32,32,128]{2,1,0:T(8,128)(2,1)S(1)}, u32[]{:S(2)}, u32[]{:S(2)}) async-start(bf16[32,32,128]{2,1,0:T(8,128)(2,1)} %attend_small.1), calls=%async_computation.3 | async-start | bytes 524288 | tf_op jit(solution)/shard_map/all_to_all | solution.py:486

commit v4 on v3

--- a/solution.py
+++ b/solution.py
@@ -18,7 +18,7 @@
 TWICE = 1.0 / SCALE
 TWICE_HIGH = float(np.asarray(TWICE, ml_dtypes.bfloat16))
 TWICE_LOW = TWICE - TWICE_HIGH
-ROWS = 256
+ROWS = 512
 CHUNK = 512
 
 
@@ -151,7 +151,13 @@
     return slice(head * HEAD_DIM, (head + 1) * HEAD_DIM)
 
 
-def prepare_first(q_ref, kv_ref, far_ref, out_ref, q_in, kv_in, staged, sems):
+def list_counts(far_ref, w, head):
+    cubes = lax.broadcasted_iota(jnp.int32, (far_ref.shape[1], HEAD_DIM), 1) % 64
+    listed = (far_ref[w, :, head : head + 1] == cubes).astype(jnp.float32)
+    return jnp.sum(listed, axis=0, keepdims=True).astype(jnp.bfloat16)
+
+
+def prepare_first(q_ref, kv_ref, far_ref, out_ref, q_in, kv_in, far_in, staged, sems, far_sem):
     groups = out_ref.shape[2]
     span = 3 * HEAD_DIM
 
@@ -165,23 +171,17 @@
     def copy_out(g):
         return pltpu.make_async_copy(staged.at[:, :, g], out_ref.at[:, :, g], sems.at[2, g])
 
+    far_copy = pltpu.make_async_copy(far_ref, far_in, far_sem)
+    far_copy.start()
     for g in range(groups):
         for copy in copies_in(g):
             copy.start()
-    cubes = lax.broadcasted_iota(jnp.int32, (far_ref.shape[1], HEAD_DIM), 1) % 64
-    top_row = lax.broadcasted_iota(jnp.int32, (8, HEAD_DIM), 0) == 0
-
-    def counts(core, head):
-        listed = far_ref[core, :, head : head + 1] == cubes
-        return jnp.sum(listed.astype(jnp.float32), axis=0, keepdims=True)
-
+    far_copy.wait()
     for g in range(groups):
         for core in range(2):
-            shared = counts(core, 3 * g + 1)
             for chip in range(2):
-                staged[chip, core, g, 256:264, :] = jnp.where(
-                    top_row, counts(core, 3 * g + 2 * chip), shared
-                ).astype(jnp.bfloat16)
+                counts = list_counts(far_in, core, 3 * g + 2 * chip)
+                staged[chip, core, g, 256:264, :] = jnp.broadcast_to(counts, (8, HEAD_DIM))
     for g in range(groups):
         for copy in copies_in(g):
             copy.wait()
@@ -197,30 +197,33 @@
         copy_out(g).wait()
 
 
-def prepare_second(q_ref, out_ref, sems):
-    copies = []
-    for g in range(out_ref.shape[2]):
-        lanes = pl.ds((3 * g + 1) * HEAD_DIM, HEAD_DIM)
-        for chip in range(2):
-            copies.append(
-                pltpu.make_async_copy(
-                    q_ref.at[:, 32 * chip : 32 * chip + 32, lanes],
-                    out_ref.at[chip, :, g],
-                    sems.at[chip, g],
-                )
-            )
+def prepare_second(q_ref, far_ref, out_ref, q_in, staged, sems, out_sem):
+    groups = out_ref.shape[0]
+    copies = [
+        pltpu.make_async_copy(
+            q_ref.at[:, :, pl.ds((3 * g + 1) * HEAD_DIM, HEAD_DIM)], q_in.at[g], sems.at[g]
+        )
+        for g in range(groups)
+    ]
     for copy in copies:
         copy.start()
-    for copy in copies:
-        copy.wait()
-
-
-def set_constants(listed, bias_ref, height_count):
-    source = lax.broadcasted_iota(jnp.int32, listed.shape, 0)
+    top_row = lax.broadcasted_iota(jnp.int32, (8, HEAD_DIM), 0) == 0
+    for g in range(groups):
+        counts = [list_counts(far_ref, w, 3 * g + 1).astype(jnp.float32) for w in range(2)]
+        staged[g, 128:136, :] = jnp.where(top_row, *counts).astype(jnp.bfloat16)
+        copies[g].wait()
+        staged[g, 0:64, :] = q_in[g, 0]
+        staged[g, 64:128, :] = q_in[g, 1]
+    copy = pltpu.make_async_copy(staged, out_ref, out_sem)
+    copy.start()
+    copy.wait()
+
+
+def set_constants(listed, time, height, bias_ref, height_count):
     lane = lax.broadcasted_iota(jnp.int32, listed.shape, 1)
     place = lane % 64 // 2
-    near = (jnp.abs(source // height_count - place // height_count) <= 1) & (
-        jnp.abs(source % height_count - place % height_count) <= 1
+    near = (jnp.abs(time - place // height_count) <= 1) & (
+        jnp.abs(height - place % height_count) <= 1
     )
     counts = listed + jnp.where(near, 1.0, 0.0)
     high = lane < 64
@@ -240,11 +243,16 @@
         kv_ref[1, s, :, :, HEAD_DIM:] = jnp.ones(shape, jnp.bfloat16)
 
 
-def attend(q_at, wait_values, kv_ref, bias_ref, out_ref, scores):
-    sources, tokens = out_ref.shape[:2]
+def attend(q_at, wait_values, kv_ref, bias_ref, out_ref, out_in, out_sems, scores):
+    sources, tokens = bias_ref.shape[0], 64
     step = ROWS // tokens
     chunk = CHUNK // 128
-    chunks = range(0, sources, chunk)
+    chunks = range(0, kv_ref.shape[1], chunk)
+    fold = out_ref.shape[1] // tokens
+
+    def copy_out(first):
+        at = pl.ds(first // fold, step // fold)
+        return pltpu.make_async_copy(out_in.at[at], out_ref.at[at], out_sems.at[first // step])
 
     def score(first, s_ref):
         bias = [
@@ -277,7 +285,9 @@
                 preferred_element_type=jnp.float32,
             )
         result = (mixed[:, :HEAD_DIM] / mixed[:, HEAD_DIM:]).astype(out_ref.dtype)
-        out_ref[pl.ds(first, step)] = result.reshape(step, tokens, HEAD_DIM)
+        at = pl.ds(first // fold, step // fold)
+        out_in[at] = result.reshape(step // fold, fold * tokens, HEAD_DIM)
+        copy_out(first).start()
 
     def two_blocks(index, largest):
         first = index * 2 * step
@@ -294,20 +304,23 @@
     later = score(last, scores[1])
     mix(last - step, scores[0], largest)
     mix(last, scores[1], later)
+    for first in range(0, sources, step):
+        copy_out(first).wait()
 
 
 def pieces(count, source, target, sems, row):
-    part = count // 4
+    part = count // 2
     return [
         pltpu.make_async_copy(
             source(pl.ds(i * part, part)), target(pl.ds(i * part, part)), sems.at[row, i]
         )
-        for i in range(4)
+        for i in range(2)
     ]
 
 
 def large_kernel(
-    height_count, mine_ref, core_ref, info_in, out_ref, kv_ref, q_in, bias_ref, sems, *scores
+    height_count, mine_ref, core_ref, info_ref, out_ref, kv_ref, q_in, info_in, out_in, bias_ref,
+    sems, out_sems, info_sem, *scores
 ):
     core = lax.axis_index("tm") % 2
     count = mine_ref.shape[0]
@@ -334,8 +347,13 @@
     query = pieces(count, lambda at: mine_ref.at[at, 0:64, :], lambda at: q_in.at[at], sems, 4)
     for copy in own[0] + other[0] + query + own[1] + other[1]:
         copy.start()
+    info_copy = pltpu.make_async_copy(info_ref, info_in, info_sem)
+    info_copy.start()
     set_margins(kv_ref)
-    set_constants(info_in[:, 0, :].astype(jnp.float32), bias_ref, height_count)
+    info_copy.wait()
+    listed = info_in[:, 0, :].astype(jnp.float32)
+    source = lax.broadcasted_iota(jnp.int32, listed.shape, 0)
+    set_constants(listed, source // height_count, source % height_count, bias_ref, height_count)
     for copy in own[0] + other[0] + query:
         copy.wait()
 
@@ -346,12 +364,12 @@
     def q_at(first, count):
         return q_in[pl.ds(first, count)].reshape(count * 64, HEAD_DIM)
 
-    attend(q_at, wait_values, kv_ref, bias_ref, out_ref, scores)
+    attend(q_at, wait_values, kv_ref, bias_ref, out_ref, out_in, out_sems, scores)
 
 
 def small_kernel(
-    height_count, first_ref, second_ref, chip_ref, core_first_ref, core_chip_ref, info_in, out_ref,
-    kv_ref, q_in, bias_ref, sems, *scores
+    height_count, first_ref, second_ref, chip_ref, core_first_ref, core_chip_ref, info_ref, out_ref,
+    kv_ref, q_in, info_in, out_in, bias_ref, sems, out_sems, info_sem, *scores
 ):
     core = lax.axis_index("tm") % 2
     chip = lax.axis_index("tm") // 2
@@ -362,22 +380,29 @@
             count, source, lambda at: kv_ref.at[kind, at, width, :, 0:HEAD_DIM], sems, row
         )
 
-    copies = pieces(count, lambda at: second_ref.at[at], lambda at: q_in.at[at], sems, 4)
+    copies = pieces(
+        height_count, lambda at: second_ref.at[at, 0:128, :], lambda at: q_in.at[at], sems, 4
+    )
     copies += kept(lambda at: first_ref.at[at, 192:256, :], chip, core, 0)
     copies += kept(lambda at: chip_ref.at[at], 1 - chip, core, 1)
     copies += kept(lambda at: core_first_ref.at[at, 192:256, :], chip, 1 - core, 2)
     copies += kept(lambda at: core_chip_ref.at[at], 1 - chip, 1 - core, 3)
     for copy in copies:
         copy.start()
+    info_copy = pltpu.make_async_copy(info_ref, info_in, info_sem)
+    info_copy.start()
     set_margins(kv_ref)
-    set_constants(info_in[:, 1, :].astype(jnp.float32), bias_ref, height_count)
+    info_copy.wait()
+    listed = info_in[:, 0:2, :].astype(jnp.float32).reshape(2 * height_count, HEAD_DIM)
+    source = lax.broadcasted_iota(jnp.int32, listed.shape, 0)
+    set_constants(listed, lax.axis_index("tm"), source // 2, bias_ref, height_count)
     for copy in copies:
         copy.wait()
 
     def q_at(first, count):
-        return q_in[pl.ds(first, count)].reshape(count * 32, HEAD_DIM)
-
-    attend(q_at, lambda: None, kv_ref, bias_ref, out_ref, scores)
+        return q_in[pl.ds(first // 2, count // 2)].reshape(count * 64, HEAD_DIM)
+
+    attend(q_at, lambda: None, kv_ref, bias_ref, out_ref, out_in, out_sems, scores)
 
 
 def side_by_side(refs, rows):
@@ -412,34 +437,38 @@
     part_ref[...] = total
 
 
-def project_small(back_ref, weight_ref, part_ref, out_ref, weights, sems):
-    groups = back_ref.shape[0] // 4
+def project_small(
+    back_ref, weight_ref, part_ref, out_ref, weights, back_in, out_in, sems, out_sems, back_sem
+):
+    groups = back_ref.shape[0]
     tiles = sems.shape[0]
     tile = weights.shape[-1]
 
-    def copies(n):
-        return [
-            pltpu.make_async_copy(
-                weight_ref.at[g, 1, :, n * tile : (n + 1) * tile], weights.at[n, g], sems.at[n, g]
-            )
-            for g in range(groups)
-        ]
-
+    def copy_in(n):
+        lanes = slice(n * tile, (n + 1) * tile)
+        return pltpu.make_async_copy(weight_ref.at[:, 1, :, lanes], weights.at[n], sems.at[n])
+
+    back_copy = pltpu.make_async_copy(back_ref, back_in, back_sem)
+    back_copy.start()
     for n in range(tiles):
-        for copy in copies(n):
-            copy.start()
-    rows = [[to * groups + g for g in range(groups)] for to in (0, 2, 1, 3)]
-    attended = side_by_side(back_ref, rows)
+        copy_in(n).start()
+    back_copy.wait()
+    attended = side_by_side(back_in, [range(groups)])
+    copies_out = []
     for n in range(tiles):
-        for copy in copies(n):
-            copy.wait()
+        copy_in(n).wait()
         lanes = slice(n * tile, (n + 1) * tile)
         total = part_ref[:, lanes] + jnp.dot(
             attended,
             weights[n].reshape(groups * HEAD_DIM, tile),
             preferred_element_type=jnp.float32,
         )
-        out_ref[:, lanes] = total.astype(out_ref.dtype)
+        out_in[:, lanes] = total.astype(out_ref.dtype)
+        copy = pltpu.make_async_copy(out_in.at[:, lanes], out_ref.at[:, lanes], out_sems.at[n])
+        copy.start()
+        copies_out.append(copy)
+    for copy in copies_out:
+        copy.wait()
 
 
 def by_heads(queries, keys_values, far_cubes, out_weight):
@@ -451,55 +480,69 @@
     far_count = far_cubes.shape[-1]
     axes = ("tm", "height")
     bf16, f32 = jnp.bfloat16, jnp.float32
-    params = pltpu.CompilerParams(vmem_limit_bytes=24 * 2**20)
+    params = pltpu.CompilerParams(vmem_limit_bytes=36 * 2**20)
     alone = pltpu.CompilerParams(vmem_limit_bytes=60 * 2**20)
     anywhere = pl.BlockSpec(memory_space=pltpu.HBM)
     queries_in = queries.reshape(2, 64, width)
     fields_in = keys_values.reshape(2, 2, 64, width)
 
+    far_lists = far_cubes.reshape(2, heads, far_count).transpose(0, 2, 1)
+
     first = pl.pallas_call(
         prepare_first,
-        in_specs=[anywhere, anywhere, pl.BlockSpec(memory_space=pltpu.VMEM)],
+        in_specs=[anywhere, anywhere, anywhere],
         out_specs=anywhere,
         out_shape=jax.ShapeDtypeStruct((2, 2, height_count, 264, HEAD_DIM), bf16),
         scratch_shapes=[
             pltpu.VMEM((height_count, 2, 64, 3 * HEAD_DIM), bf16),
             pltpu.VMEM((height_count, 2, 2, 64, 3 * HEAD_DIM), bf16),
+            pltpu.VMEM((2, far_count, heads), jnp.int32),
             pltpu.VMEM((2, 2, height_count, 264, HEAD_DIM), bf16),
             pltpu.SemaphoreType.DMA((3, height_count)),
+            pltpu.SemaphoreType.DMA,
         ],
         compiler_params=alone,
         name="prepare_first",
-    )(queries_in, fields_in, far_cubes.reshape(2, heads, far_count).transpose(0, 2, 1))
+    )(queries_in, fields_in, far_lists)
     second = pl.pallas_call(
         prepare_second,
-        in_specs=[anywhere],
+        in_specs=[anywhere, pl.BlockSpec(memory_space=pltpu.VMEM)],
         out_specs=anywhere,
-        out_shape=jax.ShapeDtypeStruct((2, 2, height_count, 32, HEAD_DIM), bf16),
-        scratch_shapes=[pltpu.SemaphoreType.DMA((2, height_count))],
+        out_shape=jax.ShapeDtypeStruct((height_count, 136, HEAD_DIM), bf16),
+        scratch_shapes=[
+            pltpu.VMEM((height_count, 2, 64, HEAD_DIM), bf16),
+            pltpu.VMEM((height_count, 136, HEAD_DIM), bf16),
+            pltpu.SemaphoreType.DMA((height_count,)),
+            pltpu.SemaphoreType.DMA,
+        ],
         compiler_params=alone,
-        cost_estimate=pl.CostEstimate(flops=0, bytes_accessed=2**20, transcendentals=0),
+        cost_estimate=pl.CostEstimate(flops=0, bytes_accessed=2**21, transcendentals=0),
         name="prepare_second",
-    )(queries_in)
-
-    def exchange(x):
-        return lax.all_to_all(x, axes, 0, 0, tiled=True)
+    )(queries_in, far_lists)
+
+    def exchange(x, over=axes):
+        return lax.all_to_all(x, over, 0, 0, tiled=True)
 
     def swap(x, distance):
         return lax.ppermute(x, "tm", [(i, i ^ distance) for i in range(tm_count)])
 
-    def attention(kernel, name, tokens, specs):
+    def attention(kernel, name, cubes, shape, operands):
         keys = devices * 128
-        work = devices * tokens * keys
+        work = cubes * 64 * keys
         return pl.pallas_call(
             functools.partial(kernel, height_count),
-            in_specs=specs,
-            out_shape=jax.ShapeDtypeStruct((devices, tokens, HEAD_DIM), bf16),
+            in_specs=[anywhere] * operands,
+            out_specs=anywhere,
+            out_shape=jax.ShapeDtypeStruct(shape, bf16),
             scratch_shapes=[
                 pltpu.VMEM((2, devices, 2, 64, 2 * HEAD_DIM), bf16),
-                pltpu.VMEM((devices, tokens, HEAD_DIM), bf16),
-                pltpu.VMEM((devices, HEAD_DIM), f32),
+                pltpu.VMEM(shape, bf16),
+                pltpu.VMEM((shape[0], 8, HEAD_DIM), bf16),
+                pltpu.VMEM(shape, bf16),
+                pltpu.VMEM((cubes, HEAD_DIM), f32),
                 pltpu.SemaphoreType.DMA((5, 4)),
+                pltpu.SemaphoreType.DMA((cubes * 64 // ROWS,)),
+                pltpu.SemaphoreType.DMA,
                 pltpu.VMEM((ROWS, keys), f32),
                 pltpu.VMEM((ROWS, keys), f32),
             ],
@@ -516,21 +559,21 @@
     small = got_first[:, 192:256]
     info = got_first[:, 256:264]
     second, small = lax.optimization_barrier((second, small))
-    got_second = exchange(second.reshape(devices, 32, HEAD_DIM))
+    got_second = exchange(second, "height")
     core_first = swap(got_first, 1)
     chip = swap(small, 2)
-    out_large = attention(large_kernel, "attend_large", 64, [anywhere, anywhere, vmem])(
+    out_large = attention(large_kernel, "attend_large", devices, (devices, 64, HEAD_DIM), 3)(
         got_first, core_first, info
     )
     core_chip = swap(chip, 1)
 
     got_second, out_large = lax.optimization_barrier((got_second, out_large))
     back_large = exchange(out_large)
-    out_small = attention(small_kernel, "attend_small", 32, [anywhere] * 5 + [vmem])(
-        got_first, got_second, chip, core_first, core_chip, info
+    out_small = attention(small_kernel, "attend_small", 2 * height_count, (height_count, 128, HEAD_DIM), 6)(
+        got_first, got_second, chip, core_first, core_chip, got_second[:, 128:136]
     )
     back_large, out_small = lax.optimization_barrier((back_large, out_small))
-    back_small = exchange(out_small)
+    back_small = exchange(out_small, "height")
     by_head = out_weight.reshape(height_count, 3, HEAD_DIM, width)
     part = pl.pallas_call(
         project_large,
@@ -549,11 +592,16 @@
     back_small, part = lax.optimization_barrier((back_small, part))
     output = pl.pallas_call(
         project_small,
-        in_specs=[vmem, anywhere, vmem],
+        in_specs=[anywhere, anywhere, vmem],
+        out_specs=anywhere,
         out_shape=jax.ShapeDtypeStruct((128, width), bf16),
         scratch_shapes=[
             pltpu.VMEM((6, height_count, HEAD_DIM, width // 6), bf16),
-            pltpu.SemaphoreType.DMA((6, height_count)),
+            pltpu.VMEM(back_small.shape, bf16),
+            pltpu.VMEM((128, width), bf16),
+            pltpu.SemaphoreType.DMA((6,)),
+            pltpu.SemaphoreType.DMA((6,)),
+            pltpu.SemaphoreType.DMA,
         ],
         compiler_params=pltpu.CompilerParams(vmem_limit_bytes=50 * 2**20),
         cost_estimate=pl.CostEstimate(

time: 120 us -> 118 us (0.983)
  Pallas kernels: 42.5 us -> 34.4 us
  waiting for transfers between devices: 56.1 us -> 61.2 us
    pallas_call x5, Pallas kernels: 37.2 us -> 29 us  [the longest x1 12 us: by_heads(): attention(large_kernel, 'attend_large', devices, (devices, 64, HEAD_DIM), 3)]
    all_to_all x4, waiting for transfers between devices: 54.3 us -> 59.3 us  [exchange(): return lax.all_to_all(x, over, 0, 0, tiled=True)]
    all_to_all x4, starting transfers between devices: 18.1 us -> 19.4 us  [exchange(): return lax.all_to_all(x, over, 0, 0, tiled=True)]
  transfers between devices with their start and end apart: 7 -> 7, of which waited for: 4 -> 4; matrix products, arithmetic and copies ran while one was open for 1% -> 1% of each run, Pallas kernels for 29% -> 23%
where the time goes in v4:
time: 118 us
  waiting for transfers between devices  61.2 us (52%)
  Pallas kernels  34.4 us (29%)
  starting transfers between devices  21 us (18%)
    all_to_all x4, waiting for transfers between devices, exchange(): return lax.all_to_all(x, over, 0, 0, tiled=True)  59.3 us
    all_to_all x4, starting transfers between devices, exchange(): return lax.all_to_all(x, over, 0, 0, tiled=True)  19.4 us
    pallas_call x1, Pallas kernels, by_heads(): attention(large_kernel, 'attend_large', devices, (devices, 64, HEAD_DIM), 3)  12 us
    pallas_call x1, Pallas kernels, by_heads(): attention(small_kernel, 'attend_small', 2 * height_count, (height_count,...  6.84 us
    pallas_call x1, Pallas kernels, by_heads(): pl.pallas_call(project_large, in_specs=[vmem, anywhere], out_shape=pltpu....  5.32 us
    pallas_call x1, Pallas kernels, by_heads(): pl.pallas_call(project_small, in_specs=[anywhere, anywhere, vmem], out_sp...  4.05 us
    pallas_call x1, Pallas kernels, by_heads(): pl.pallas_call(prepare_first, in_specs=[anywhere, anywhere, anywhere], ou...  3.25 us
    pallas_call x1, Pallas kernels, by_heads(): pl.pallas_call(prepare_second, in_specs=[anywhere, pl.BlockSpec(memory_sp...  2.87 us
  transfers between devices with their start and end apart: 7, of which 4 were waited for; matrix products, arithmetic and copies ran while one was open for 1% of the time, Pallas kernels for 23%

profile of v4, /device:TPU:0, one launch (start us, length us, event | category | flops | bytes accessed | tf_op | source)
XLA Modules:
  0.0 117.6 jit_solution(9636803331446880679)
XLA Ops:
  0.0 3.3 %prepare_first.1 = bf16[2,2,8,264,128]{4,3,2,1,0:T(8,128)(2,1)} custom-call(bf16[2,64,3072]{2,1,0:T(8,128)(2,1)} %bitcast.11, bf16[2,2,64,3072]{3,2,1,0:T(8,128)(2,1)} %bitcast.13, s32[2,16,24]{2,1,0:T(8,128)} %bitcast.14), custom_call_target="tpu_custom_call" | custom-call | tf_op jit(solution)/shard_map/prepare_first/pallas_call | solution.py:491
  3.3 7.3 %all-to-all-start = ((bf16[32,264,128]{2,1,0:T(8,128)(2,1)}), bf16[32,264,128]{2,1,0:T(8,128)(2,1)S(1)}, u32[]{:S(2)}, u32[]{:S(2)}) async-start(bf16[32,264,128]{2,1,0:T(8,128)(2,1)} %bitcast.10), calls=%async_computation | async-start | bytes 4325376 | tf_op jit(solution)/shard_map/all_to_all | solution.py:524
  10.6 2.9 %prepare_second.1 = bf16[8,136,128]{2,1,0:T(8,128)(2,1)} custom-call(bf16[2,64,3072]{2,1,0:T(8,128)(2,1)} %bitcast.12, s32[2,16,24]{2,1,0:T(8,128)} %bitcast.15), custom_call_target="tpu_custom_call" | custom-call | bytes 2097152 | tf_op jit(solution)/shard_map/prepare_second/pallas_call | solution.py:507
  13.4 48.6 %all-to-all-done.mine_ref.first_ref = bf16[32,264,128]{2,1,0:T(8,128)(2,1)S(1)} async-done(((bf16[32,264,128]{2,1,0:T(8,128)(2,1)}), bf16[32,264,128]{2,1,0:T(8,128)(2,1)S(1)}, u32[]{:S(2)}, u32[]{:S(2)}) %all-to-all-start) | async-done | bytes 2162720 | tf_op jit(solution)/shard_map/all_to_all | solution.py:524
  62.1 0.0 collective-permute-start
  62.1 0.9 slice.9
  63.0 3.4 %all-to-all-start.1 = ((bf16[8,136,128]{2,1,0:T(8,128)(2,1)}), bf16[8,136,128]{2,1,0:T(8,128)(2,1)S(1)}, u32[]{:S(2)}, u32[]{:S(2)}) async-start(bf16[8,136,128]{2,1,0:T(8,128)(2,1)} %prepare_second.1), calls=%async_computation.1 | async-start | bytes 557056 | tf_op jit(solution)/shard_map/all_to_all | solution.py:524
  66.4 1.4 %collective-permute-start.1 = (bf16[32,64,128]{2,1,0:T(8,128)(2,1)}, bf16[32,64,128]{2,1,0:T(8,128)(2,1)S(1)}, u32[]{:S(2)}, u32[]{:S(2)}) collective-permute-start(bf16[32,64,128]{2,1,0:T(8,128)(2,1)} %slice.9), channel_id=1, source_target_pairs={{0,16},{8,24},{16,0},{24,8},{1,17},{9,25},{17,1},{25,9},{2,18},{10... | collective-permute-start | bytes 1572872 | tf_op jit(solution)/shard_map/ppermute | solution.py:527
  67.8 0.0 collective-permute-done.core_ref.core_first_ref
  67.8 12.0 %attend_large.1 = bf16[32,64,128]{2,1,0:T(8,128)(2,1)} custom-call(bf16[32,264,128]{2,1,0:T(8,128)(2,1)S(1)} %all-to-all-done.mine_ref.first_ref, bf16[32,264,128]{2,1,0:T(8,128)(2,1)} %collective-permute-done.core_ref.core_first_ref, bf16[32,8,128]{2,1,0:T(8,128)(2,1)S(1)} %slice.10.info_ref), custom_call_target="tpu_custom_call" | custom-call | flops 8589934592 | bytes 4194304 | tf_op jit(solution)/shard_map/attend_large/pallas_call | solution.py:565
  79.8 0.0 all-to-all-done.1.second_ref
  79.8 5.3 %all-to-all-start.2 = ((bf16[32,64,128]{2,1,0:T(8,128)(2,1)}), bf16[32,64,128]{2,1,0:T(8,128)(2,1)S(1)}, u32[]{:S(2)}, u32[]{:S(2)}) async-start(bf16[32,64,128]{2,1,0:T(8,128)(2,1)} %attend_large.1), calls=%async_computation.2 | async-start | bytes 1048576 | tf_op jit(solution)/shard_map/all_to_all | solution.py:524
  85.1 0.0 collective-permute-done.1.chip_ref
  85.1 0.1 collective-permute-start.2
  85.3 1.8 %collective-permute-done.2.core_chip_ref = bf16[32,64,128]{2,1,0:T(8,128)(2,1)S(1)} collective-permute-done((bf16[32,64,128]{2,1,0:T(8,128)(2,1)S(1)}, bf16[32,64,128]{2,1,0:T(8,128)(2,1)S(1)}, u32[]{:S(2)}, u32[]{:S(2)}) %collective-permute-start.2) | collective-permute-done | bytes 524320 | tf_op jit(solution)/shard_map/ppermute | solution.py:527
  87.1 6.8 %attend_small.1 = bf16[8,128,128]{2,1,0:T(8,128)(2,1)} custom-call(bf16[32,264,128]{2,1,0:T(8,128)(2,1)S(1)} %all-to-all-done.mine_ref.first_ref, bf16[8,136,128]{2,1,0:T(8,128)(2,1)S(1)} %all-to-all-done.1.second_ref, bf16[32,64,128]{2,1,0:T(8,128)(2,1)S(1)} %collective-permute-done.1.chip_ref, ...), custom_call_target="tpu_custom_call" | custom-call | flops 4294967296 | bytes 4194304 | tf_op jit(solution)/shard_map/attend_small/pallas_call | solution.py:572
  94.0 7.3 %all-to-all-done.2.back_ref = bf16[32,64,128]{2,1,0:T(8,128)(2,1)S(1)} async-done(((bf16[32,64,128]{2,1,0:T(8,128)(2,1)}), bf16[32,64,128]{2,1,0:T(8,128)(2,1)S(1)}, u32[]{:S(2)}, u32[]{:S(2)}) %all-to-all-start.2) | async-done | bytes 524320 | tf_op jit(solution)/shard_map/all_to_all | solution.py:524
  101.3 3.4 %all-to-all-start.3 = ((bf16[8,128,128]{2,1,0:T(8,128)(2,1)}), bf16[8,128,128]{2,1,0:T(8,128)(2,1)S(1)}, u32[]{:S(2)}, u32[]{:S(2)}) async-start(bf16[8,128,128]{2,1,0:T(8,128)(2,1)} %attend_small.1), calls=%async_computation.3 | async-start | bytes 524288 | tf_op jit(solution)/shard_map/all_to_all | solution.py:524
  104.7 5.3 %project_large.1.part_ref = f32[128,3072]{1,0:T(8,128)S(1)} custom-call(bf16[32,64,128]{2,1,0:T(8,128)(2,1)S(1)} %all-to-all-done.2.back_ref, bf16[8,3,128,3072]{3,2,1,0:T(8,128)(2,1)} %bitcast.8), custom_call_target="tpu_custom_call" | custom-call | flops 1610612736 | bytes 14680064 | tf_op jit(solution)/shard_map/project_large/pallas_call | solution.py:578
  110.0 3.3 %all-to-all-done.3.back_ref = bf16[8,128,128]{2,1,0:T(8,128)(2,1)S(1)} async-done(((bf16[8,128,128]{2,1,0:T(8,128)(2,1)}), bf16[8,128,128]{2,1,0:T(8,128)(2,1)S(1)}, u32[]{:S(2)}, u32[]{:S(2)}) %all-to-all-start.3) | async-done | bytes 262176 | tf_op jit(solution)/shard_map/all_to_all | solution.py:524
  113.4 4.0 %project_small.1 = bf16[128,3072]{1,0:T(8,128)(2,1)} custom-call(bf16[8,128,128]{2,1,0:T(8,128)(2,1)S(1)} %all-to-all-done.3.back_ref, bf16[8,3,128,3072]{3,2,1,0:T(8,128)(2,1)} %bitcast.9, f32[128,3072]{1,0:T(8,128)S(1)} %project_large.1.part_ref), custom_call_target="tpu_custom_call" | custom-call | flops 805306368 | bytes 8388608 | tf_op jit(solution)/shard_map/project_small/pallas_call | solution.py:593
  (2 shorter events, 0.0 us)
Async XLA Ops:
  3.3 58.8 %all-to-all-start = ((bf16[32,264,128]{2,1,0:T(8,128)(2,1)}), bf16[32,264,128]{2,1,0:T(8,128)(2,1)S(1)}, u32[]{:S(2)}, u32[]{:S(2)}) async-start(bf16[32,264,128]{2,1,0:T(8,128)(2,1)} %bitcast.10), calls=%async_computation | async-start | bytes 4325376 | tf_op jit(solution)/shard_map/all_to_all | solution.py:524
  62.1 5.7 %collective-permute-start = (bf16[32,264,128]{2,1,0:T(8,128)(2,1)S(1)}, bf16[32,264,128]{2,1,0:T(8,128)(2,1)}, u32[]{:S(2)}, u32[]{:S(2)}) collective-permute-start(bf16[32,264,128]{2,1,0:T(8,128)(2,1)S(1)} %all-to-all-done.mine_ref.first_ref), channel_id=1, source_target_pairs={{0,8},{8,0},{16,24},{24,16},{1,9},{9,1},{17,25},{25,17},{2,10},{10... | collective-permute-start | bytes 6488072 | tf_op jit(solution)/shard_map/ppermute | solution.py:527
  63.0 16.9 %all-to-all-start.1 = ((bf16[8,136,128]{2,1,0:T(8,128)(2,1)}), bf16[8,136,128]{2,1,0:T(8,128)(2,1)S(1)}, u32[]{:S(2)}, u32[]{:S(2)}) async-start(bf16[8,136,128]{2,1,0:T(8,128)(2,1)} %prepare_second.1), calls=%async_computation.1 | async-start | bytes 557056 | tf_op jit(solution)/shard_map/all_to_all | solution.py:524
  66.4 18.7 %collective-permute-start.1 = (bf16[32,64,128]{2,1,0:T(8,128)(2,1)}, bf16[32,64,128]{2,1,0:T(8,128)(2,1)S(1)}, u32[]{:S(2)}, u32[]{:S(2)}) collective-permute-start(bf16[32,64,128]{2,1,0:T(8,128)(2,1)} %slice.9), channel_id=1, source_target_pairs={{0,16},{8,24},{16,0},{24,8},{1,17},{9,25},{17,1},{25,9},{2,18},{10... | collective-permute-start | bytes 1572872 | tf_op jit(solution)/shard_map/ppermute | solution.py:527
  79.8 21.5 %all-to-all-start.2 = ((bf16[32,64,128]{2,1,0:T(8,128)(2,1)}), bf16[32,64,128]{2,1,0:T(8,128)(2,1)S(1)}, u32[]{:S(2)}, u32[]{:S(2)}) async-start(bf16[32,64,128]{2,1,0:T(8,128)(2,1)} %attend_large.1), calls=%async_computation.2 | async-start | bytes 1048576 | tf_op jit(solution)/shard_map/all_to_all | solution.py:524
  85.1 2.0 %collective-permute-start.2 = (bf16[32,64,128]{2,1,0:T(8,128)(2,1)S(1)}, bf16[32,64,128]{2,1,0:T(8,128)(2,1)S(1)}, u32[]{:S(2)}, u32[]{:S(2)}) collective-permute-start(bf16[32,64,128]{2,1,0:T(8,128)(2,1)S(1)} %collective-permute-done.1.chip_ref), channel_id=1, source_target_pairs={{0,8},{8,0},{16,24},{24,16},{1,9},{9,1},{17,25},{25,17},{2,10},{10... | collective-permute-start | bytes 1572872 | tf_op jit(solution)/shard_map/ppermute | solution.py:527
  101.3 12.1 %all-to-all-start.3 = ((bf16[8,128,128]{2,1,0:T(8,128)(2,1)}), bf16[8,128,128]{2,1,0:T(8,128)(2,1)S(1)}, u32[]{:S(2)}, u32[]{:S(2)}) async-start(bf16[8,128,128]{2,1,0:T(8,128)(2,1)} %attend_small.1), calls=%async_computation.3 | async-start | bytes 524288 | tf_op jit(solution)/shard_map/all_to_all | solution.py:524

commit v5 on v4

--- a/solution.py
+++ b/solution.py
@@ -159,42 +159,44 @@
 
 def prepare_first(q_ref, kv_ref, far_ref, out_ref, q_in, kv_in, far_in, staged, sems, far_sem):
     groups = out_ref.shape[2]
-    span = 3 * HEAD_DIM
-
-    def copies_in(g):
-        lanes = pl.ds(g * span, span)
-        return (
-            pltpu.make_async_copy(q_ref.at[:, :, lanes], q_in.at[g], sems.at[0, g]),
-            pltpu.make_async_copy(kv_ref.at[:, :, :, lanes], kv_in.at[g], sems.at[1, g]),
-        )
-
-    def copy_out(g):
-        return pltpu.make_async_copy(staged.at[:, :, g], out_ref.at[:, :, g], sems.at[2, g])
+
+    def copies_in(core):
+        return [
+            pltpu.make_async_copy(q_ref.at[core], q_in.at[core], sems.at[core, 0]),
+            pltpu.make_async_copy(kv_ref.at[core, 0], kv_in.at[core, 0], sems.at[core, 1]),
+            pltpu.make_async_copy(kv_ref.at[core, 1], kv_in.at[core, 1], sems.at[core, 2]),
+        ]
+
+    def copy_out(chip, core):
+        return pltpu.make_async_copy(
+            staged.at[chip, core], out_ref.at[chip, core], sems.at[core, 3 + chip]
+        )
 
     far_copy = pltpu.make_async_copy(far_ref, far_in, far_sem)
     far_copy.start()
-    for g in range(groups):
-        for copy in copies_in(g):
+    for core in range(2):
+        for copy in copies_in(core):
             copy.start()
     far_copy.wait()
-    for g in range(groups):
-        for core in range(2):
-            for chip in range(2):
+    for core in range(2):
+        for chip in range(2):
+            for g in range(groups):
                 counts = list_counts(far_in, core, 3 * g + 2 * chip)
                 staged[chip, core, g, 256:264, :] = jnp.broadcast_to(counts, (8, HEAD_DIM))
-    for g in range(groups):
-        for copy in copies_in(g):
+    for core in range(2):
+        for copy in copies_in(core):
             copy.wait()
-        for core in range(2):
-            for chip in range(2):
-                lanes = head_lanes(2 * chip)
-                staged[chip, core, g, 0:64, :] = q_in[g, core, :, lanes]
-                staged[chip, core, g, 64:128, :] = kv_in[g, core, 0, :, lanes]
-                staged[chip, core, g, 128:192, :] = kv_in[g, core, 1, :, lanes]
-                staged[chip, core, g, 192:256, :] = kv_in[g, core, chip, :, head_lanes(1)]
-        copy_out(g).start()
-    for g in range(groups):
-        copy_out(g).wait()
+        for chip in range(2):
+            for g in range(groups):
+                lanes = head_lanes(3 * g + 2 * chip)
+                staged[chip, core, g, 0:64, :] = q_in[core, :, lanes]
+                staged[chip, core, g, 64:128, :] = kv_in[core, 0, :, lanes]
+                staged[chip, core, g, 128:192, :] = kv_in[core, 1, :, lanes]
+                staged[chip, core, g, 192:256, :] = kv_in[core, chip, :, head_lanes(3 * g + 1)]
+            copy_out(chip, core).start()
+    for core in range(2):
+        for chip in range(2):
+            copy_out(chip, core).wait()
 
 
 def prepare_second(q_ref, far_ref, out_ref, q_in, staged, sems, out_sem):
@@ -494,11 +496,11 @@
         out_specs=anywhere,
         out_shape=jax.ShapeDtypeStruct((2, 2, height_count, 264, HEAD_DIM), bf16),
         scratch_shapes=[
-            pltpu.VMEM((height_count, 2, 64, 3 * HEAD_DIM), bf16),
-            pltpu.VMEM((height_count, 2, 2, 64, 3 * HEAD_DIM), bf16),
+            pltpu.VMEM((2, 64, width), bf16),
+            pltpu.VMEM((2, 2, 64, width), bf16),
             pltpu.VMEM((2, far_count, heads), jnp.int32),
             pltpu.VMEM((2, 2, height_count, 264, HEAD_DIM), bf16),
-            pltpu.SemaphoreType.DMA((3, height_count)),
+            pltpu.SemaphoreType.DMA((2, 5)),
             pltpu.SemaphoreType.DMA,
         ],
         compiler_params=alone,

time: 118 us -> 118 us (level)
  no operation moved by 1% of the time
where the time goes in v5:
time: 118 us; the launch traced here: 117 us
  waiting for transfers between devices  61.2 us (52%)
  Pallas kernels  34.1 us (29%)
  starting transfers between devices  21 us (18%)
    all_to_all x4, waiting for transfers between devices, exchange(): return lax.all_to_all(x, over, 0, 0, tiled=True)  59.3 us
    all_to_all x4, starting transfers between devices, exchange(): return lax.all_to_all(x, over, 0, 0, tiled=True)  19.4 us
    pallas_call x1, Pallas kernels, by_heads(): attention(large_kernel, 'attend_large', devices, (devices, 64, HEAD_DIM), 3)  12 us
    pallas_call x1, Pallas kernels, by_heads(): attention(small_kernel, 'attend_small', 2 * height_count, (height_count,...  6.85 us
    pallas_call x1, Pallas kernels, by_heads(): pl.pallas_call(project_large, in_specs=[vmem, anywhere], out_shape=pltpu....  5.31 us
    pallas_call x1, Pallas kernels, by_heads(): pl.pallas_call(project_small, in_specs=[anywhere, anywhere, vmem], out_sp...  4.05 us
    pallas_call x1, Pallas kernels, by_heads(): pl.pallas_call(prepare_first, in_specs=[anywhere, anywhere, anywhere], ou...  3.02 us
    pallas_call x1, Pallas kernels, by_heads(): pl.pallas_call(prepare_second, in_specs=[anywhere, pl.BlockSpec(memory_sp...  2.87 us
  transfers between devices with their start and end apart: 7, of which 4 were waited for; matrix products, arithmetic and copies ran while one was open for 1% of the time, Pallas kernels for 23%

profile of v5, /device:TPU:0, one launch (start us, length us, event | category | flops | bytes accessed | tf_op | source)
XLA Modules:
  0.0 117.4 jit_solution(13462450413158942089)
XLA Ops:
  0.0 3.0 %prepare_first.1 = bf16[2,2,8,264,128]{4,3,2,1,0:T(8,128)(2,1)} custom-call(bf16[2,64,3072]{2,1,0:T(8,128)(2,1)} %bitcast.11, bf16[2,2,64,3072]{3,2,1,0:T(8,128)(2,1)} %bitcast.13, s32[2,16,24]{2,1,0:T(8,128)} %bitcast.14), custom_call_target="tpu_custom_call" | custom-call | tf_op jit(solution)/shard_map/prepare_first/pallas_call | solution.py:493
  3.0 7.3 %all-to-all-start = ((bf16[32,264,128]{2,1,0:T(8,128)(2,1)}), bf16[32,264,128]{2,1,0:T(8,128)(2,1)S(1)}, u32[]{:S(2)}, u32[]{:S(2)}) async-start(bf16[32,264,128]{2,1,0:T(8,128)(2,1)} %bitcast.10), calls=%async_computation | async-start | bytes 4325376 | tf_op jit(solution)/shard_map/all_to_all | solution.py:526
  10.3 2.9 %prepare_second.1 = bf16[8,136,128]{2,1,0:T(8,128)(2,1)} custom-call(bf16[2,64,3072]{2,1,0:T(8,128)(2,1)} %bitcast.12, s32[2,16,24]{2,1,0:T(8,128)} %bitcast.15), custom_call_target="tpu_custom_call" | custom-call | bytes 2097152 | tf_op jit(solution)/shard_map/prepare_second/pallas_call | solution.py:509
  13.2 48.6 %all-to-all-done.mine_ref.first_ref = bf16[32,264,128]{2,1,0:T(8,128)(2,1)S(1)} async-done(((bf16[32,264,128]{2,1,0:T(8,128)(2,1)}), bf16[32,264,128]{2,1,0:T(8,128)(2,1)S(1)}, u32[]{:S(2)}, u32[]{:S(2)}) %all-to-all-start) | async-done | bytes 2162720 | tf_op jit(solution)/shard_map/all_to_all | solution.py:526
  61.9 0.0 collective-permute-start
  61.9 0.9 slice.9
  62.7 3.4 %all-to-all-start.1 = ((bf16[8,136,128]{2,1,0:T(8,128)(2,1)}), bf16[8,136,128]{2,1,0:T(8,128)(2,1)S(1)}, u32[]{:S(2)}, u32[]{:S(2)}) async-start(bf16[8,136,128]{2,1,0:T(8,128)(2,1)} %prepare_second.1), calls=%async_computation.1 | async-start | bytes 557056 | tf_op jit(solution)/shard_map/all_to_all | solution.py:526
  66.1 1.4 %collective-permute-start.1 = (bf16[32,64,128]{2,1,0:T(8,128)(2,1)}, bf16[32,64,128]{2,1,0:T(8,128)(2,1)S(1)}, u32[]{:S(2)}, u32[]{:S(2)}) collective-permute-start(bf16[32,64,128]{2,1,0:T(8,128)(2,1)} %slice.9), channel_id=1, source_target_pairs={{0,16},{8,24},{16,0},{24,8},{1,17},{9,25},{17,1},{25,9},{2,18},{10... | collective-permute-start | bytes 1572872 | tf_op jit(solution)/shard_map/ppermute | solution.py:529
  67.5 0.0 collective-permute-done.core_ref.core_first_ref
  67.5 12.0 %attend_large.1 = bf16[32,64,128]{2,1,0:T(8,128)(2,1)} custom-call(bf16[32,264,128]{2,1,0:T(8,128)(2,1)S(1)} %all-to-all-done.mine_ref.first_ref, bf16[32,264,128]{2,1,0:T(8,128)(2,1)} %collective-permute-done.core_ref.core_first_ref, bf16[32,8,128]{2,1,0:T(8,128)(2,1)S(1)} %slice.10.info_ref), custom_call_target="tpu_custom_call" | custom-call | flops 8589934592 | bytes 4194304 | tf_op jit(solution)/shard_map/attend_large/pallas_call | solution.py:567
  79.6 0.0 all-to-all-done.1.second_ref
  79.6 5.3 %all-to-all-start.2 = ((bf16[32,64,128]{2,1,0:T(8,128)(2,1)}), bf16[32,64,128]{2,1,0:T(8,128)(2,1)S(1)}, u32[]{:S(2)}, u32[]{:S(2)}) async-start(bf16[32,64,128]{2,1,0:T(8,128)(2,1)} %attend_large.1), calls=%async_computation.2 | async-start | bytes 1048576 | tf_op jit(solution)/shard_map/all_to_all | solution.py:526
  84.9 0.0 collective-permute-done.1.chip_ref
  84.9 0.1 collective-permute-start.2
  85.0 1.8 %collective-permute-done.2.core_chip_ref = bf16[32,64,128]{2,1,0:T(8,128)(2,1)S(1)} collective-permute-done((bf16[32,64,128]{2,1,0:T(8,128)(2,1)S(1)}, bf16[32,64,128]{2,1,0:T(8,128)(2,1)S(1)}, u32[]{:S(2)}, u32[]{:S(2)}) %collective-permute-start.2) | collective-permute-done | bytes 524320 | tf_op jit(solution)/shard_map/ppermute | solution.py:529
  86.9 6.8 %attend_small.1 = bf16[8,128,128]{2,1,0:T(8,128)(2,1)} custom-call(bf16[32,264,128]{2,1,0:T(8,128)(2,1)S(1)} %all-to-all-done.mine_ref.first_ref, bf16[8,136,128]{2,1,0:T(8,128)(2,1)S(1)} %all-to-all-done.1.second_ref, bf16[32,64,128]{2,1,0:T(8,128)(2,1)S(1)} %collective-permute-done.1.chip_ref, ...), custom_call_target="tpu_custom_call" | custom-call | flops 4294967296 | bytes 4194304 | tf_op jit(solution)/shard_map/attend_small/pallas_call | solution.py:574
  93.7 7.3 %all-to-all-done.2.back_ref = bf16[32,64,128]{2,1,0:T(8,128)(2,1)S(1)} async-done(((bf16[32,64,128]{2,1,0:T(8,128)(2,1)}), bf16[32,64,128]{2,1,0:T(8,128)(2,1)S(1)}, u32[]{:S(2)}, u32[]{:S(2)}) %all-to-all-start.2) | async-done | bytes 524320 | tf_op jit(solution)/shard_map/all_to_all | solution.py:526
  101.1 3.4 %all-to-all-start.3 = ((bf16[8,128,128]{2,1,0:T(8,128)(2,1)}), bf16[8,128,128]{2,1,0:T(8,128)(2,1)S(1)}, u32[]{:S(2)}, u32[]{:S(2)}) async-start(bf16[8,128,128]{2,1,0:T(8,128)(2,1)} %attend_small.1), calls=%async_computation.3 | async-start | bytes 524288 | tf_op jit(solution)/shard_map/all_to_all | solution.py:526
  104.5 5.3 %project_large.1.part_ref = f32[128,3072]{1,0:T(8,128)S(1)} custom-call(bf16[32,64,128]{2,1,0:T(8,128)(2,1)S(1)} %all-to-all-done.2.back_ref, bf16[8,3,128,3072]{3,2,1,0:T(8,128)(2,1)} %bitcast.8), custom_call_target="tpu_custom_call" | custom-call | flops 1610612736 | bytes 14680064 | tf_op jit(solution)/shard_map/project_large/pallas_call | solution.py:580
  109.8 3.3 %all-to-all-done.3.back_ref = bf16[8,128,128]{2,1,0:T(8,128)(2,1)S(1)} async-done(((bf16[8,128,128]{2,1,0:T(8,128)(2,1)}), bf16[8,128,128]{2,1,0:T(8,128)(2,1)S(1)}, u32[]{:S(2)}, u32[]{:S(2)}) %all-to-all-start.3) | async-done | bytes 262176 | tf_op jit(solution)/shard_map/all_to_all | solution.py:526
  113.1 4.1 %project_small.1 = bf16[128,3072]{1,0:T(8,128)(2,1)} custom-call(bf16[8,128,128]{2,1,0:T(8,128)(2,1)S(1)} %all-to-all-done.3.back_ref, bf16[8,3,128,3072]{3,2,1,0:T(8,128)(2,1)} %bitcast.9, f32[128,3072]{1,0:T(8,128)S(1)} %project_large.1.part_ref), custom_call_target="tpu_custom_call" | custom-call | flops 805306368 | bytes 8388608 | tf_op jit(solution)/shard_map/project_small/pallas_call | solution.py:595
  (2 shorter events, 0.0 us)
Async XLA Ops:
  3.0 58.8 %all-to-all-start = ((bf16[32,264,128]{2,1,0:T(8,128)(2,1)}), bf16[32,264,128]{2,1,0:T(8,128)(2,1)S(1)}, u32[]{:S(2)}, u32[]{:S(2)}) async-start(bf16[32,264,128]{2,1,0:T(8,128)(2,1)} %bitcast.10), calls=%async_computation | async-start | bytes 4325376 | tf_op jit(solution)/shard_map/all_to_all | solution.py:526
  61.9 5.7 %collective-permute-start = (bf16[32,264,128]{2,1,0:T(8,128)(2,1)S(1)}, bf16[32,264,128]{2,1,0:T(8,128)(2,1)}, u32[]{:S(2)}, u32[]{:S(2)}) collective-permute-start(bf16[32,264,128]{2,1,0:T(8,128)(2,1)S(1)} %all-to-all-done.mine_ref.first_ref), channel_id=1, source_target_pairs={{0,8},{8,0},{16,24},{24,16},{1,9},{9,1},{17,25},{25,17},{2,10},{10... | collective-permute-start | bytes 6488072 | tf_op jit(solution)/shard_map/ppermute | solution.py:529
  62.7 16.9 %all-to-all-start.1 = ((bf16[8,136,128]{2,1,0:T(8,128)(2,1)}), bf16[8,136,128]{2,1,0:T(8,128)(2,1)S(1)}, u32[]{:S(2)}, u32[]{:S(2)}) async-start(bf16[8,136,128]{2,1,0:T(8,128)(2,1)} %prepare_second.1), calls=%async_computation.1 | async-start | bytes 557056 | tf_op jit(solution)/shard_map/all_to_all | solution.py:526
  66.1 18.7 %collective-permute-start.1 = (bf16[32,64,128]{2,1,0:T(8,128)(2,1)}, bf16[32,64,128]{2,1,0:T(8,128)(2,1)S(1)}, u32[]{:S(2)}, u32[]{:S(2)}) collective-permute-start(bf16[32,64,128]{2,1,0:T(8,128)(2,1)} %slice.9), channel_id=1, source_target_pairs={{0,16},{8,24},{16,0},{24,8},{1,17},{9,25},{17,1},{25,9},{2,18},{10... | collective-permute-start | bytes 1572872 | tf_op jit(solution)/shard_map/ppermute | solution.py:529
  79.6 21.5 %all-to-all-start.2 = ((bf16[32,64,128]{2,1,0:T(8,128)(2,1)}), bf16[32,64,128]{2,1,0:T(8,128)(2,1)S(1)}, u32[]{:S(2)}, u32[]{:S(2)}) async-start(bf16[32,64,128]{2,1,0:T(8,128)(2,1)} %attend_large.1), calls=%async_computation.2 | async-start | bytes 1048576 | tf_op jit(solution)/shard_map/all_to_all | solution.py:526
  84.9 2.0 %collective-permute-start.2 = (bf16[32,64,128]{2,1,0:T(8,128)(2,1)S(1)}, bf16[32,64,128]{2,1,0:T(8,128)(2,1)S(1)}, u32[]{:S(2)}, u32[]{:S(2)}) collective-permute-start(bf16[32,64,128]{2,1,0:T(8,128)(2,1)S(1)} %collective-permute-done.1.chip_ref), channel_id=1, source_target_pairs={{0,8},{8,0},{16,24},{24,16},{1,9},{9,1},{17,25},{25,17},{2,10},{10... | collective-permute-start | bytes 1572872 | tf_op jit(solution)/shard_map/ppermute | solution.py:529
  101.1 12.1 %all-to-all-start.3 = ((bf16[8,128,128]{2,1,0:T(8,128)(2,1)}), bf16[8,128,128]{2,1,0:T(8,128)(2,1)S(1)}, u32[]{:S(2)}, u32[]{:S(2)}) async-start(bf16[8,128,128]{2,1,0:T(8,128)(2,1)} %attend_small.1), calls=%async_computation.3 | async-start | bytes 524288 | tf_op jit(solution)/shard_map/all_to_all | solution.py:526

commit v6 on v5

--- a/solution.py
+++ b/solution.py
@@ -183,7 +183,6 @@
             for g in range(groups):
                 counts = list_counts(far_in, core, 3 * g + 2 * chip)
                 staged[chip, core, g, 256:264, :] = jnp.broadcast_to(counts, (8, HEAD_DIM))
-    for core in range(2):
         for copy in copies_in(core):
             copy.wait()
         for chip in range(2):

time: 118 us -> 118 us (level)
  no operation moved by 1% of the time
where the time goes in v6:
time: 118 us; the launch traced here: 117 us
  waiting for transfers between devices  61.2 us (52%)
  Pallas kernels  34.1 us (29%)
  starting transfers between devices  21 us (18%)
    all_to_all x4, waiting for transfers between devices, exchange(): return lax.all_to_all(x, over, 0, 0, tiled=True)  59.3 us
    all_to_all x4, starting transfers between devices, exchange(): return lax.all_to_all(x, over, 0, 0, tiled=True)  19.4 us
    pallas_call x1, Pallas kernels, by_heads(): attention(large_kernel, 'attend_large', devices, (devices, 64, HEAD_DIM), 3)  12 us
    pallas_call x1, Pallas kernels, by_heads(): attention(small_kernel, 'attend_small', 2 * height_count, (height_count,...  6.85 us
    pallas_call x1, Pallas kernels, by_heads(): pl.pallas_call(project_large, in_specs=[vmem, anywhere], out_shape=pltpu....  5.31 us
    pallas_call x1, Pallas kernels, by_heads(): pl.pallas_call(project_small, in_specs=[anywhere, anywhere, vmem], out_sp...  4.05 us
    pallas_call x1, Pallas kernels, by_heads(): pl.pallas_call(prepare_first, in_specs=[anywhere, anywhere, anywhere], ou...  2.97 us
    pallas_call x1, Pallas kernels, by_heads(): pl.pallas_call(prepare_second, in_specs=[anywhere, pl.BlockSpec(memory_sp...  2.87 us
  transfers between devices with their start and end apart: 7, of which 4 were waited for; matrix products, arithmetic and copies ran while one was open for 1% of the time, Pallas kernels for 23%

profile of v6, /device:TPU:0, one launch (start us, length us, event | category | flops | bytes accessed | tf_op | source)
XLA Modules:
  0.0 117.3 jit_solution(4924424951721790472)
XLA Ops:
  0.0 3.0 %prepare_first.1 = bf16[2,2,8,264,128]{4,3,2,1,0:T(8,128)(2,1)} custom-call(bf16[2,64,3072]{2,1,0:T(8,128)(2,1)} %bitcast.11, bf16[2,2,64,3072]{3,2,1,0:T(8,128)(2,1)} %bitcast.13, s32[2,16,24]{2,1,0:T(8,128)} %bitcast.14), custom_call_target="tpu_custom_call" | custom-call | tf_op jit(solution)/shard_map/prepare_first/pallas_call | solution.py:492
  3.0 7.3 %all-to-all-start = ((bf16[32,264,128]{2,1,0:T(8,128)(2,1)}), bf16[32,264,128]{2,1,0:T(8,128)(2,1)S(1)}, u32[]{:S(2)}, u32[]{:S(2)}) async-start(bf16[32,264,128]{2,1,0:T(8,128)(2,1)} %bitcast.10), calls=%async_computation | async-start | bytes 4325376 | tf_op jit(solution)/shard_map/all_to_all | solution.py:525
  10.3 2.9 %prepare_second.1 = bf16[8,136,128]{2,1,0:T(8,128)(2,1)} custom-call(bf16[2,64,3072]{2,1,0:T(8,128)(2,1)} %bitcast.12, s32[2,16,24]{2,1,0:T(8,128)} %bitcast.15), custom_call_target="tpu_custom_call" | custom-call | bytes 2097152 | tf_op jit(solution)/shard_map/prepare_second/pallas_call | solution.py:508
  13.2 48.6 %all-to-all-done.mine_ref.first_ref = bf16[32,264,128]{2,1,0:T(8,128)(2,1)S(1)} async-done(((bf16[32,264,128]{2,1,0:T(8,128)(2,1)}), bf16[32,264,128]{2,1,0:T(8,128)(2,1)S(1)}, u32[]{:S(2)}, u32[]{:S(2)}) %all-to-all-start) | async-done | bytes 2162720 | tf_op jit(solution)/shard_map/all_to_all | solution.py:525
  61.8 0.0 collective-permute-start
  61.8 0.9 slice.9
  62.7 3.4 %all-to-all-start.1 = ((bf16[8,136,128]{2,1,0:T(8,128)(2,1)}), bf16[8,136,128]{2,1,0:T(8,128)(2,1)S(1)}, u32[]{:S(2)}, u32[]{:S(2)}) async-start(bf16[8,136,128]{2,1,0:T(8,128)(2,1)} %prepare_second.1), calls=%async_computation.1 | async-start | bytes 557056 | tf_op jit(solution)/shard_map/all_to_all | solution.py:525
  66.1 1.4 %collective-permute-start.1 = (bf16[32,64,128]{2,1,0:T(8,128)(2,1)}, bf16[32,64,128]{2,1,0:T(8,128)(2,1)S(1)}, u32[]{:S(2)}, u32[]{:S(2)}) collective-permute-start(bf16[32,64,128]{2,1,0:T(8,128)(2,1)} %slice.9), channel_id=1, source_target_pairs={{0,16},{8,24},{16,0},{24,8},{1,17},{9,25},{17,1},{25,9},{2,18},{10... | collective-permute-start | bytes 1572872 | tf_op jit(solution)/shard_map/ppermute | solution.py:528
  67.5 0.0 collective-permute-done.core_ref.core_first_ref
  67.5 12.0 %attend_large.1 = bf16[32,64,128]{2,1,0:T(8,128)(2,1)} custom-call(bf16[32,264,128]{2,1,0:T(8,128)(2,1)S(1)} %all-to-all-done.mine_ref.first_ref, bf16[32,264,128]{2,1,0:T(8,128)(2,1)} %collective-permute-done.core_ref.core_first_ref, bf16[32,8,128]{2,1,0:T(8,128)(2,1)S(1)} %slice.10.info_ref), custom_call_target="tpu_custom_call" | custom-call | flops 8589934592 | bytes 4194304 | tf_op jit(solution)/shard_map/attend_large/pallas_call | solution.py:566
  79.5 0.0 all-to-all-done.1.second_ref
  79.5 5.3 %all-to-all-start.2 = ((bf16[32,64,128]{2,1,0:T(8,128)(2,1)}), bf16[32,64,128]{2,1,0:T(8,128)(2,1)S(1)}, u32[]{:S(2)}, u32[]{:S(2)}) async-start(bf16[32,64,128]{2,1,0:T(8,128)(2,1)} %attend_large.1), calls=%async_computation.2 | async-start | bytes 1048576 | tf_op jit(solution)/shard_map/all_to_all | solution.py:525
  84.8 0.0 collective-permute-done.1.chip_ref
  84.8 0.1 collective-permute-start.2
  85.0 1.8 %collective-permute-done.2.core_chip_ref = bf16[32,64,128]{2,1,0:T(8,128)(2,1)S(1)} collective-permute-done((bf16[32,64,128]{2,1,0:T(8,128)(2,1)S(1)}, bf16[32,64,128]{2,1,0:T(8,128)(2,1)S(1)}, u32[]{:S(2)}, u32[]{:S(2)}) %collective-permute-start.2) | collective-permute-done | bytes 524320 | tf_op jit(solution)/shard_map/ppermute | solution.py:528
  86.8 6.8 %attend_small.1 = bf16[8,128,128]{2,1,0:T(8,128)(2,1)} custom-call(bf16[32,264,128]{2,1,0:T(8,128)(2,1)S(1)} %all-to-all-done.mine_ref.first_ref, bf16[8,136,128]{2,1,0:T(8,128)(2,1)S(1)} %all-to-all-done.1.second_ref, bf16[32,64,128]{2,1,0:T(8,128)(2,1)S(1)} %collective-permute-done.1.chip_ref, ...), custom_call_target="tpu_custom_call" | custom-call | flops 4294967296 | bytes 4194304 | tf_op jit(solution)/shard_map/attend_small/pallas_call | solution.py:573
  93.7 7.3 %all-to-all-done.2.back_ref = bf16[32,64,128]{2,1,0:T(8,128)(2,1)S(1)} async-done(((bf16[32,64,128]{2,1,0:T(8,128)(2,1)}), bf16[32,64,128]{2,1,0:T(8,128)(2,1)S(1)}, u32[]{:S(2)}, u32[]{:S(2)}) %all-to-all-start.2) | async-done | bytes 524320 | tf_op jit(solution)/shard_map/all_to_all | solution.py:525
  101.0 3.4 %all-to-all-start.3 = ((bf16[8,128,128]{2,1,0:T(8,128)(2,1)}), bf16[8,128,128]{2,1,0:T(8,128)(2,1)S(1)}, u32[]{:S(2)}, u32[]{:S(2)}) async-start(bf16[8,128,128]{2,1,0:T(8,128)(2,1)} %attend_small.1), calls=%async_computation.3 | async-start | bytes 524288 | tf_op jit(solution)/shard_map/all_to_all | solution.py:525
  104.4 5.3 %project_large.1.part_ref = f32[128,3072]{1,0:T(8,128)S(1)} custom-call(bf16[32,64,128]{2,1,0:T(8,128)(2,1)S(1)} %all-to-all-done.2.back_ref, bf16[8,3,128,3072]{3,2,1,0:T(8,128)(2,1)} %bitcast.8), custom_call_target="tpu_custom_call" | custom-call | flops 1610612736 | bytes 14680064 | tf_op jit(solution)/shard_map/project_large/pallas_call | solution.py:579
  109.7 3.3 %all-to-all-done.3.back_ref = bf16[8,128,128]{2,1,0:T(8,128)(2,1)S(1)} async-done(((bf16[8,128,128]{2,1,0:T(8,128)(2,1)}), bf16[8,128,128]{2,1,0:T(8,128)(2,1)S(1)}, u32[]{:S(2)}, u32[]{:S(2)}) %all-to-all-start.3) | async-done | bytes 262176 | tf_op jit(solution)/shard_map/all_to_all | solution.py:525
  113.1 4.1 %project_small.1 = bf16[128,3072]{1,0:T(8,128)(2,1)} custom-call(bf16[8,128,128]{2,1,0:T(8,128)(2,1)S(1)} %all-to-all-done.3.back_ref, bf16[8,3,128,3072]{3,2,1,0:T(8,128)(2,1)} %bitcast.9, f32[128,3072]{1,0:T(8,128)S(1)} %project_large.1.part_ref), custom_call_target="tpu_custom_call" | custom-call | flops 805306368 | bytes 8388608 | tf_op jit(solution)/shard_map/project_small/pallas_call | solution.py:594
  (2 shorter events, 0.0 us)
Async XLA Ops:
  3.0 58.8 %all-to-all-start = ((bf16[32,264,128]{2,1,0:T(8,128)(2,1)}), bf16[32,264,128]{2,1,0:T(8,128)(2,1)S(1)}, u32[]{:S(2)}, u32[]{:S(2)}) async-start(bf16[32,264,128]{2,1,0:T(8,128)(2,1)} %bitcast.10), calls=%async_computation | async-start | bytes 4325376 | tf_op jit(solution)/shard_map/all_to_all | solution.py:525
  61.8 5.7 %collective-permute-start = (bf16[32,264,128]{2,1,0:T(8,128)(2,1)S(1)}, bf16[32,264,128]{2,1,0:T(8,128)(2,1)}, u32[]{:S(2)}, u32[]{:S(2)}) collective-permute-start(bf16[32,264,128]{2,1,0:T(8,128)(2,1)S(1)} %all-to-all-done.mine_ref.first_ref), channel_id=1, source_target_pairs={{0,8},{8,0},{16,24},{24,16},{1,9},{9,1},{17,25},{25,17},{2,10},{10... | collective-permute-start | bytes 6488072 | tf_op jit(solution)/shard_map/ppermute | solution.py:528
  62.7 16.9 %all-to-all-start.1 = ((bf16[8,136,128]{2,1,0:T(8,128)(2,1)}), bf16[8,136,128]{2,1,0:T(8,128)(2,1)S(1)}, u32[]{:S(2)}, u32[]{:S(2)}) async-start(bf16[8,136,128]{2,1,0:T(8,128)(2,1)} %prepare_second.1), calls=%async_computation.1 | async-start | bytes 557056 | tf_op jit(solution)/shard_map/all_to_all | solution.py:525
  66.1 18.7 %collective-permute-start.1 = (bf16[32,64,128]{2,1,0:T(8,128)(2,1)}, bf16[32,64,128]{2,1,0:T(8,128)(2,1)S(1)}, u32[]{:S(2)}, u32[]{:S(2)}) collective-permute-start(bf16[32,64,128]{2,1,0:T(8,128)(2,1)} %slice.9), channel_id=1, source_target_pairs={{0,16},{8,24},{16,0},{24,8},{1,17},{9,25},{17,1},{25,9},{2,18},{10... | collective-permute-start | bytes 1572872 | tf_op jit(solution)/shard_map/ppermute | solution.py:528
  79.5 21.5 %all-to-all-start.2 = ((bf16[32,64,128]{2,1,0:T(8,128)(2,1)}), bf16[32,64,128]{2,1,0:T(8,128)(2,1)S(1)}, u32[]{:S(2)}, u32[]{:S(2)}) async-start(bf16[32,64,128]{2,1,0:T(8,128)(2,1)} %attend_large.1), calls=%async_computation.2 | async-start | bytes 1048576 | tf_op jit(solution)/shard_map/all_to_all | solution.py:525
  84.8 2.0 %collective-permute-start.2 = (bf16[32,64,128]{2,1,0:T(8,128)(2,1)S(1)}, bf16[32,64,128]{2,1,0:T(8,128)(2,1)S(1)}, u32[]{:S(2)}, u32[]{:S(2)}) collective-permute-start(bf16[32,64,128]{2,1,0:T(8,128)(2,1)S(1)} %collective-permute-done.1.chip_ref), channel_id=1, source_target_pairs={{0,8},{8,0},{16,24},{24,16},{1,9},{9,1},{17,25},{25,17},{2,10},{10... | collective-permute-start | bytes 1572872 | tf_op jit(solution)/shard_map/ppermute | solution.py:528
  101.0 12.1 %all-to-all-start.3 = ((bf16[8,128,128]{2,1,0:T(8,128)(2,1)}), bf16[8,128,128]{2,1,0:T(8,128)(2,1)S(1)}, u32[]{:S(2)}, u32[]{:S(2)}) async-start(bf16[8,128,128]{2,1,0:T(8,128)(2,1)} %attend_small.1), calls=%async_computation.3 | async-start | bytes 524288 | tf_op jit(solution)/shard_map/all_to_all | solution.py:525
